TPU v7x, 512 devices: a whole 4x4x16 slice. The times are simulated.
512 devices in a mesh: dp: 64 (over z, y_hi, core), tensor: 8 (over y_lo, x).
Axes of the slice: x: 4, y: 4 (y_hi: 2, y_lo: 2; y = y_hi * 2 + y_lo), z: 16, core: 2. Of those that a mesh axis runs over, the one named last changes fastest.
Arguments:
- tokens: bfloat16 [8192, 8192], P('dp', 'tensor'), may hold values from -6 to 6
- frozen_gate_up: bfloat16 [8192, 2, 15360], P('dp', None, 'tensor'), may hold values from -6 to 6
- frozen_down_factor: bfloat16 [4, 64, 8192], P(None, None, 'tensor'), may hold values from -0.0625 to 0.0625
- prior_b_factors: float32 [4, 2, 15360, 64], P(None, None, ('tensor', 'dp')), may hold values from -2 to 2
- first_moment_owned: float32 [4, 2, 15360, 64], P(None, None, ('tensor', 'dp')), may hold values from -6 to 6
- second_moment_owned: float32 [4, 2, 15360, 64], P(None, None, ('tensor', 'dp')), may hold values from 0.5 to 8
- replica_gradients: bfloat16 [64, 4, 2, 15360, 64], P('dp', None, None, 'tensor'), may hold values from -16 to 16
- adapter_of_block: int32 [64, 1], replicated, may hold values from 0 to 3
- live_row_count: int32 [64, 1], replicated, may hold values from 32 to 128
- owner_block_table: int32 [64], replicated, may hold values from 0 to 63, each once
Outputs:
- new_b: float32 [4, 2, 15360, 64], P(None, None, ('tensor', 'dp'))
- new_m: float32 [4, 2, 15360, 64], P(None, None, ('tensor', 'dp'))
- new_v: float32 [4, 2, 15360, 64], P(None, None, ('tensor', 'dp'))
- hidden: bfloat16 [8192, 15360], P('dp', 'tensor')
All inputs are finite; a program needn't handle non-finite values.
Results may differ from a plain program's by a relative error of at most 0.0067.
Values may be sent and summed in bfloat16 or wider, within the bound.
A program may use at most 128 MiB of HBM per device.

v0:
```python
import jax
import jax.numpy as jnp
from jax import lax
from jax.sharding import PartitionSpec as P

ADAM_STEP = 20


ADAPTER_SCALE = 2.0
BETA_ONE = 0.9
BETA_TWO = 0.95
LEARN_RATE = 0.05
EPSILON = 1e-08


def owner_inverse(owner_block_table):
    count = owner_block_table.shape[0]
    iota = jnp.arange(count, dtype=jnp.int32)
    return jnp.sum(jnp.where(owner_block_table[None, :] == iota[:, None], iota[None, :], 0), axis=1)


def on_device(
    tokens,
    frozen_gate_up,
    frozen_down_factor,
    prior_b_factors,
    first_moment_owned,
    second_moment_owned,
    replica_gradients,
    adapter_of_block,
    live_row_count,
    owner_block_table,
):
    n_owners = lax.axis_size("dp")
    my_index = lax.axis_index("dp")
    adapters, _, owned_rows, rank = prior_b_factors.shape
    local_hidden_width = owned_rows * n_owners
    row_total = tokens.shape[0]
    row_blocks = adapter_of_block.shape[1]
    row_block = row_total // row_blocks
    adapter_labels = lax.dynamic_index_in_dim(adapter_of_block, my_index, 0, keepdims=False)
    counts = lax.dynamic_index_in_dim(live_row_count, my_index, 0, keepdims=False)
    inverse = owner_inverse(owner_block_table)
    parts = replica_gradients.reshape(adapters, 2, n_owners, owned_rows, rank)
    ordered = (
        parts[:, :, owner_block_table]
        .reshape(adapters, 2, local_hidden_width, rank)
        .astype(jnp.float32)
    )
    grad_total = lax.psum_scatter(ordered, "dp", scatter_dimension=2, tiled=True)
    prior = prior_b_factors.astype(jnp.bfloat16)
    everyone = lax.all_gather(prior, "dp", axis=2, tiled=True)
    natural = everyone.reshape(adapters, 2, n_owners, owned_rows, rank)[:, :, inverse]
    chosen = natural.reshape(adapters, 2, local_hidden_width, rank)[adapter_labels]
    grouped_rows = tokens.reshape(row_blocks, row_block, tokens.shape[1])
    partial_value = jnp.einsum(
        "aok,afk->aof",
        grouped_rows,
        frozen_down_factor[adapter_labels],
        preferred_element_type=jnp.float32,
    )
    shrunk = lax.psum(partial_value, "tensor").astype(jnp.bfloat16)
    adapter_change = jnp.einsum(
        "bnr,bcgr->bncg", shrunk, chosen, preferred_element_type=jnp.float32
    )
    gate_up_activations = (
        frozen_gate_up.reshape(row_blocks, row_block, 2, local_hidden_width).astype(jnp.float32)
        + ADAPTER_SCALE * adapter_change
    )
    gated = jax.nn.silu(gate_up_activations[:, :, 0]) * gate_up_activations[:, :, 1]
    live = jnp.arange(row_block, dtype=jnp.int32)[None, :] < counts[:, None]
    hidden = (
        jnp.where(live[:, :, None], gated, jnp.float32(0.0))
        .astype(jnp.bfloat16)
        .reshape(row_total, local_hidden_width)
    )
    new_m = BETA_ONE * first_moment_owned + (1.0 - BETA_ONE) * grad_total
    new_v = BETA_TWO * second_moment_owned + (1.0 - BETA_TWO) * grad_total * grad_total
    m_hat = new_m / (1.0 - BETA_ONE**ADAM_STEP)
    v_hat = new_v / (1.0 - BETA_TWO**ADAM_STEP)
    new_b = prior_b_factors - LEARN_RATE * m_hat / (jnp.sqrt(v_hat) + EPSILON)
    return (new_b, new_m, new_v, hidden)


def solution(mesh):
    placed = (
        P("dp", "tensor"),
        P("dp", None, "tensor"),
        P(None, None, "tensor"),
        P(None, None, ("tensor", "dp"), None),
        P(None, None, ("tensor", "dp"), None),
        P(None, None, ("tensor", "dp"), None),
        P("dp", None, None, "tensor", None),
        P(),
        P(),
        P(),
    )
    return jax.shard_map(
        on_device,
        mesh=mesh,
        in_specs=placed,
        out_specs=(
            P(None, None, ("tensor", "dp"), None),
            P(None, None, ("tensor", "dp"), None),
            P(None, None, ("tensor", "dp"), None),
            P("dp", "tensor"),
        ),
        check_vma=False,
    )
```

profile of v0, /device:TPU:1, one launch (start us, length us, event | category | flops | bytes accessed | tf_op | source)
XLA Modules:
  0.0 727.8 jit_solution(14295065480500331804)
XLA Ops:
  7.2 1.6 convert_element_type.26
  8.9 8.8 %copy.42 = bf16[1,4,2,1920,64]{4,2,3,1,0:T(2,128)(2,1)} copy(bf16[1,4,2,1920,64]{3,4,2,1,0:T(8,128)(2,1)} %param.16) | data formatting | bytes 3932160 | tf_op args[6]
  17.8 7.0 copy.43
  24.8 8.3 %gather_fusion = bf16[64,4,2,30,64]{4,1,3,2,0:T(4,128)(2,1)} fusion(bf16[4,2,64,30,64]{4,0,3,2,1:T(4,128)(2,1)} %copy.43, s32[1024]{0:T(1024)S(1)} %pad_clamp_fusion.1), kind=kCustom, calls=%fused_computation | custom fusion | bytes 3932416 | tf_op jit(solution)/shard_map/gather | solution.py:46
  33.1 6.2 convert_bitcast_fusion
  39.3 10.4 %copy.44 = f32[4,2,64,30,64]{4,1,3,2,0:T(2,128)} copy(f32[4,2,64,30,64]{4,0,3,1,2:T(4,128)} %convert_bitcast_fusion) | data formatting | bytes 7864320 | tf_op jit(solution)/shard_map/convert_element_type | solution.py:48
  49.8 11.2 %copy.45 = f32[4,2,1920,64]{3,0,1,2:T(4,128)} copy(f32[4,2,1920,64]{3,1,2,0:T(2,128)} %bitcast.44) | data formatting | bytes 7864320 | tf_op jit(solution)/shard_map/convert_element_type | solution.py:48
  61.0 0.6 copy-done.6
  61.7 0.6 constant_dynamic-slice_fusion.1
  63.6 1.3 dynamic-slice.8
  66.4 28.1 %psum.7 = bf16[1,128,64]{1,2,0:T(8,128)(2,1)S(1)} all-reduce(f32[1,128,64]{1,2,0:T(8,128)S(1)} %convolution_bitcast_fusion), channel_id=1, replica_groups=mesh['dp'=64,'tensor'=8] {'tensor'}, use_global_device_ids=true, to_apply=%region_1.2 | all-reduce | flops 8192 | bytes 49152 | tf_op jit(solution)/shard_map/psum | solution.py:62
  94.5 0.6 iota_compare_fusion.1
  95.3 71.8 %all-gather.2.cloned.1.call-done = bf16[4,2,1920,64]{3,1,2,0:T(2,128)(2,1)} async-done(((bf16[4,2,30,64]{3,1,2,0:T(2,128)(2,1)}), bf16[4,2,1920,64]{3,1,2,0:T(2,128)(2,1)}) %all-gather.2.cloned.1.call-update) | async-done | bytes 1966096 | tf_op jit(solution)/shard_map/all_gather | solution.py:52
  167.0 7.2 copy.49
  174.3 8.3 %gather_fusion.1 = bf16[64,4,2,30,64]{4,1,3,2,0:T(4,128)(2,1)} fusion(bf16[4,2,64,30,64]{4,0,3,2,1:T(4,128)(2,1)} %bitcast.45, s32[1024]{0:T(1024)S(1)} %pad_clamp_fusion), kind=kCustom, calls=%fused_computation.1 | custom fusion | bytes 3932416 | tf_op jit(solution)/shard_map/gather | solution.py:53
  182.6 5.2 copy.50
  187.9 0.7 constant_dynamic-slice_fusion
  188.6 0.7 copy.51
  189.8 1.1 fusion.4
  190.9 526.9 %all-reduce.3.cloned.1.call-done = f32[4,2,1920,64]{3,0,1,2:T(4,128)} async-done(((f32[4,2,1920,64]{3,0,1,2:T(4,128)}), f32[4,2,1920,64]{3,0,1,2:T(4,128)}) %all-reduce.3.cloned.1.call-update) | async-done | bytes 3932176
  717.8 1.1 copy_subtract_fusion
  718.9 0.7 copy.52
  719.6 0.7 copy.53
  720.3 0.7 copy.54
  (28 shorter events, 0.9 us)
Async XLA Ops:
  7.2 59.0 %copy-start = (bf16[4,64,1024]{2,1,0:T(8,128)(2,1)S(1)}, bf16[4,64,1024]{2,1,0:T(8,128)(2,1)}, u32[]{:S(2)}) copy-start(bf16[4,64,1024]{2,1,0:T(8,128)(2,1)} %param.12) | copy-start | bytes 1572868
  7.2 159.9 %all-gather.2.cloned.1.call-start = ((), (), s32[]{:S(2)}) async-start(), calls=%async_computation | async-start | bytes 3993600 | tf_op jit(solution)/shard_map/all_gather | solution.py:52
  8.9 708.9 %all-reduce.3.cloned.1.call-start = ((), (), s32[]{:S(2)}) async-start(), calls=%async_computation.1 | async-start | bytes 15728640
  17.8 7.0 copy-start.8
  61.0 0.7 copy-start.6
  61.0 0.7 copy-start.7
  61.0 5.1 copy-start.3
  182.6 6.7 copy-start.1
  188.6 529.1 %copy-start.2 = (f32[4,2,30,64]{3,1,2,0:T(2,128)S(1)}, f32[4,2,30,64]{3,1,2,0:T(2,128)}, u32[]{:S(2)}) copy-start(f32[4,2,30,64]{3,1,2,0:T(2,128)} %param.13) | copy-start | bytes 184324
  188.6 529.1 %copy-start.4 = (f32[4,2,30,64]{3,1,2,0:T(2,128)S(1)}, f32[4,2,30,64]{3,1,2,0:T(2,128)}, u32[]{:S(2)}) copy-start(f32[4,2,30,64]{3,1,2,0:T(2,128)} %param.14) | copy-start | bytes 184324
  188.6 529.1 %copy-start.5 = (f32[4,2,30,64]{3,1,2,0:T(2,128)S(1)}, f32[4,2,30,64]{3,1,2,0:T(2,128)}, u32[]{:S(2)}) copy-start(f32[4,2,30,64]{3,1,2,0:T(2,128)} %param.15) | copy-start | bytes 184324
Sparse Core Ops, SparseCore 0:
  11.8 155.1 all-gather.1
  170.0 547.7 all-reduce.2
where the time goes:
time: 729 us; the launch traced here: 728 us
  waiting for transfers between devices  599 us (82%)
  local copies, waits for them, and re-layouts  72.7 us (10%)
  blocking collectives  28.1 us (4%)
  between operations  16.8 us (2%)
  other arithmetic  10.9 us (1%)
    unnamed x3, waiting for transfers between devices  527 us
    all_gather x1, waiting for transfers between devices, on_device(): everyone = lax.all_gather(prior, 'dp', axis=2, tiled=True)  71.8 us
    psum x1, blocking collectives, on_device(): shrunk = lax.psum(partial_value, 'tensor').astype(jnp.bfloat16)  28.1 us
    convert_element_type x2, local copies, waits for them, and re-layouts, on_device(): ordered = parts[:, :, owner_block_table].reshape(adapters, 2, local_hidde...  21.7 us
  transfers between devices with their start and end apart: 2, of which 2 were waited for; matrix products, arithmetic and copies ran while one was open for 11% of the time, Pallas kernels for 0%

commit v1 on v0

v1 whole, which is shorter than its diff:
```python
import functools

import jax
import jax.numpy as jnp
from jax import lax
from jax.experimental import pallas as pl
from jax.experimental.pallas import tpu as pltpu
from jax.sharding import PartitionSpec as P

ADAM_STEP = 20


ADAPTER_SCALE = 2.0
BETA_ONE = 0.9
BETA_TWO = 0.95
LEARN_RATE = 0.05
EPSILON = 1e-08

MESH = pl.DeviceIdType.MESH
Z = 16
PLANE = 4
TENSOR = 8
UP = Z // 2 - 1
DOWN = Z // 2
STEPS = Z // 2
FB = 30
PAD = 32
LANES = 128
WIRE = jnp.bfloat16
F32 = jnp.float32
BF16 = jnp.bfloat16


def owner_inverse(owner_block_table):
    count = owner_block_table.shape[0]
    iota = jnp.arange(count, dtype=jnp.int32)
    return jnp.sum(jnp.where(owner_block_table[None, :] == iota[:, None], iota[None, :], 0), axis=1)


def slots_of_batch(step):
    if step == 0:
        return 0, 3
    if step == STEPS - 1:
        return 2 * step + 1, 1
    return 2 * step + 1, 2


def exchange_kernel(
    adapters_ref,
    table_ref,
    inverse_ref,
    tokens_ref,
    down_ref,
    mine_ref,
    grads_ref,
    bt_ref,
    shrunk_ref,
    total_ref,
    own_half,
    other_half,
    terms,
    up_out,
    up_in,
    down_out,
    down_in,
    gather_up,
    gather_down,
    spread_out,
    spread_in,
    final_out,
    final_in,
    partial_sums,
    natural,
    local_sem,
    half_send,
    half_recv,
    up_send,
    up_recv,
    down_send,
    down_recv,
    gup_send,
    gup_recv,
    gdown_send,
    gdown_recv,
    spread_send,
    spread_recv,
    final_send,
    final_recv,
    psum_send,
    psum_recv,
):
    dp = lax.axis_index("dp")
    tensor = lax.axis_index("tensor")
    z = dp // PLANE
    plane = dp % PLANE
    core = plane % 2
    base = z * PLANE
    above = (lax.rem(z + 1, Z) * PLANE + plane, tensor)
    below = (lax.rem(z + Z - 1, Z) * PLANE + plane, tensor)
    sibling = (base + plane - core + (1 - core), tensor)
    mates = [lax.rem(plane + step, PLANE) for step in range(1, PLANE)]
    mate_ids = [(base + mate, tensor) for mate in mates]
    peers = [lax.rem(tensor + step, TENSOR) for step in range(1, TENSOR)]
    peer_ids = [(dp, peer) for peer in peers]

    own_copies = [
        pltpu.make_async_copy(grads_ref.at[2 * core + p], own_half.at[p], local_sem.at[p])
        for p in range(2)
    ]
    for copy in own_copies:
        copy.start()

    barrier = pltpu.get_barrier_semaphore()
    everyone = [above, below] + mate_ids + peer_ids
    for device in everyone:
        pl.semaphore_signal(barrier, inc=1, device_id=device, device_id_type=MESH)

    my_adapter = adapters_ref[dp]
    partial_sums[tensor] = lax.dot_general(
        down_ref[my_adapter],
        tokens_ref[...],
        (((1,), (1,)), ((), ())),
        preferred_element_type=F32,
    )
    plane_adapters = [adapters_ref[base + lax.rem(plane + step, PLANE)] for step in range(PLANE)]

    pl.semaphore_wait(barrier, len(everyone))

    def remote(src, dst, send, recv, device):
        return pltpu.make_async_remote_copy(
            src_ref=src,
            dst_ref=dst,
            send_sem=send,
            recv_sem=recv,
            device_id=device,
            device_id_type=MESH,
        )

    halves = [
        remote(
            grads_ref.at[2 * (1 - core) + p],
            other_half.at[p],
            half_send.at[p],
            half_recv.at[p],
            sibling,
        )
        for p in range(2)
    ]
    for copy in halves:
        copy.start()

    def go_up(step):
        source = mine_ref if step == 0 else gather_up.at[step - 1]
        return remote(source, gather_up.at[step], gup_send.at[step], gup_recv.at[step], above)

    def go_down(step):
        source = mine_ref if step == 0 else gather_down.at[step - 1]
        return remote(source, gather_down.at[step], gdown_send.at[step], gdown_recv.at[step], below)

    gups = [go_up(step) for step in range(DOWN)]
    gdowns = [go_down(step) for step in range(UP)]
    gups[0].start()
    gdowns[0].start()

    psums = [
        remote(
            partial_sums.at[tensor],
            partial_sums.at[tensor],
            psum_send.at[i],
            psum_recv.at[tensor],
            device,
        )
        for i, device in enumerate(peer_ids)
    ]
    for copy in psums:
        copy.start()

    def picker(q):
        window = jnp.minimum((120 * q) // LANES * LANES, 1920 - 2 * LANES)
        offset = 120 * q - window
        row = lax.broadcasted_iota(jnp.int32, (PLANE * PAD, 2 * LANES), 0)
        column = lax.broadcasted_iota(jnp.int32, (PLANE * PAD, 2 * LANES), 1)
        hit = (column == offset + row - 2 * (row // PAD)) & (row % PAD < FB)
        return pl.multiple_of(window, LANES), jnp.where(hit, F32(1.0), F32(0.0)).astype(BF16)

    def turned(half, p, window, pick):
        block = lax.dot_general(
            pick,
            half[p, :, pl.ds(window, 2 * LANES)],
            (((1,), (1,)), ((), ())),
            preferred_element_type=F32,
        )
        return block.reshape(PLANE, PAD, LANES)

    for copy in own_copies:
        copy.wait()

    @pl.loop(0, Z)
    def _(q):
        window, pick = picker(q)
        for p in range(2):
            terms[pl.ds(PLANE * q, PLANE), p] = turned(own_half, p, window, pick)

    for copy in halves:
        copy.wait_recv()

    @pl.loop(0, Z)
    def _(q):
        window, pick = picker(q)
        for p in range(2):
            terms[pl.ds(PLANE * q, PLANE), p] += turned(other_half, p, window, pick)

    def term(target, p, b):
        return terms[table_ref[PLANE * target + b], p]

    def send_up(step, p):
        return remote(
            up_out.at[step, p], up_in.at[step, p], up_send.at[step, p], up_recv.at[step, p], above
        )

    def send_down(step, p):
        return remote(
            down_out.at[step, p],
            down_in.at[step, p],
            down_send.at[step, p],
            down_recv.at[step, p],
            below,
        )

    ups = [[send_up(step, p) for p in range(2)] for step in range(UP)]
    downs = [[send_down(step, p) for p in range(2)] for step in range(DOWN)]

    def spread(step, i):
        first, count = slots_of_batch(step)
        return remote(
            spread_out.at[i, pl.ds(first, count)],
            spread_in.at[plane, pl.ds(first, count)],
            spread_send.at[step, i],
            spread_recv.at[step, plane],
            mate_ids[i],
        )

    def choose(block, adapter):
        result = block[0]
        for a in range(1, 4):
            result = jnp.where(adapter == a, block[a], result)
        return result

    spreads = []
    for step in range(STEPS):
        for p in range(2):
            if step < UP:
                target = lax.rem(z + UP - step, Z)
                if step > 0:
                    ups[step - 1][p].wait_recv()
                for b in range(PLANE):
                    value = term(target, p, b)
                    if step > 0:
                        value = value + up_in[step - 1, p, b].astype(F32)
                    up_out[step, p, b] = value.astype(WIRE)
                ups[step][p].start()
            target = lax.rem(z + Z - DOWN + step, Z)
            if step > 0:
                downs[step - 1][p].wait_recv()
            for b in range(PLANE):
                value = term(target, p, b)
                if step > 0:
                    value = value + down_in[step - 1, p, b].astype(F32)
                down_out[step, p, b] = value.astype(WIRE)
            downs[step][p].start()

        arrived = []
        if step == 0:
            arrived.append(mine_ref[...])
        gups[step].wait_recv()
        if step + 1 < DOWN:
            gups[step + 1].start()
        arrived.append(gather_up[step])
        if step < UP:
            gdowns[step].wait_recv()
            if step + 1 < UP:
                gdowns[step + 1].start()
            arrived.append(gather_down[step])
        first, count = slots_of_batch(step)
        for n in range(count):
            spread_in[plane, first + n] = choose(arrived[n], plane_adapters[0])
            for i in range(PLANE - 1):
                spread_out[i, first + n] = choose(arrived[n], plane_adapters[i + 1])
        for i in range(PLANE - 1):
            copy = spread(step, i)
            copy.start()
            spreads.append(copy)

    for p in range(2):
        ups[UP - 1][p].wait_recv()
        downs[DOWN - 1][p].wait_recv()
        for b in range(PLANE):
            value = (
                term(z, p, b)
                + up_in[UP - 1, p, b].astype(F32)
                + down_in[DOWN - 1, p, b].astype(F32)
            )
            final_out[b, p] = value
    finals = [
        remote(
            final_out.at[mate],
            final_in.at[plane],
            final_send.at[i],
            final_recv.at[plane],
            mate_ids[i],
        )
        for i, mate in enumerate(mates)
    ]
    for copy in finals:
        copy.start()
    final_in[plane] = final_out[plane]

    for peer in peers:
        remote(
            partial_sums.at[peer],
            partial_sums.at[peer],
            psum_send.at[0],
            psum_recv.at[peer],
            peer_ids[0],
        ).wait_recv()
    shrunk = partial_sums[0]
    for i in range(1, TENSOR):
        shrunk = shrunk + partial_sums[i]
    shrunk_ref[...] = shrunk.astype(BF16)

    for step in range(STEPS):
        first, count = slots_of_batch(step)
        for i, mate in enumerate(mates):
            remote(
                spread_out.at[i, pl.ds(first, count)],
                spread_in.at[mate, pl.ds(first, count)],
                spread_send.at[step, i],
                spread_recv.at[step, mate],
                mate_ids[i],
            ).wait_recv()

    @pl.loop(0, Z * PLANE)
    def _(k):
        owner = inverse_ref[k]
        delta = lax.rem(owner // PLANE - z + Z, Z)
        slot = jnp.where(delta < STEPS, 2 * delta, 2 * Z - 1 - 2 * delta)
        natural[k] = spread_in[owner % PLANE, slot]

    @pl.loop(0, 1920 // LANES)
    def _(t):
        first = jnp.minimum((LANES * t) // FB, Z * PLANE - 6)
        offset = LANES * t - FB * first
        row = lax.broadcasted_iota(jnp.int32, (6 * PAD, LANES), 0)
        column = lax.broadcasted_iota(jnp.int32, (6 * PAD, LANES), 1)
        hit = (row - 2 * (row // PAD) == offset + column) & (row % PAD < FB)
        pick = jnp.where(hit, F32(1.0), F32(0.0)).astype(BF16)
        block = lax.dot_general(
            natural[pl.ds(first, 6)].reshape(6 * PAD, LANES),
            pick,
            (((0,), (0,)), ((), ())),
            preferred_element_type=F32,
        )
        bt_ref[:, pl.ds(pl.multiple_of(t * LANES, LANES), LANES)] = block.astype(BF16)

    for i, mate in enumerate(mates):
        remote(
            final_out.at[mate],
            final_in.at[mate],
            final_send.at[i],
            final_recv.at[mate],
            mate_ids[i],
        ).wait_recv()
    for c in range(2):
        for p in range(2):
            total_ref[2 * c + p] = final_in[c, p] + final_in[2 + c, p]

    for copy in halves + gups + gdowns + psums + spreads + finals:
        copy.wait_send()
    for pair in ups + downs:
        for copy in pair:
            copy.wait_send()


def exchange(adapters, table, inverse, tokens, down, mine, grads):
    smem = pl.BlockSpec(memory_space=pltpu.SMEM)
    vmem = pl.BlockSpec(memory_space=pltpu.VMEM)
    dma = pltpu.SemaphoreType.DMA
    chunk = (PLANE, PAD, LANES)
    return pl.pallas_call(
        exchange_kernel,
        out_shape=(
            jax.ShapeDtypeStruct((LANES, 1920), BF16),
            jax.ShapeDtypeStruct((64, 128), BF16),
            jax.ShapeDtypeStruct((4, PAD, LANES), F32),
        ),
        in_specs=[smem, smem, smem, vmem, vmem, vmem, pl.BlockSpec(memory_space=pl.ANY)],
        out_specs=(vmem, vmem, vmem),
        scratch_shapes=[
            pltpu.VMEM((2, LANES, 1920), BF16),
            pltpu.VMEM((2, LANES, 1920), BF16),
            pltpu.VMEM((Z * PLANE, 2, PAD, LANES), F32),
            pltpu.VMEM((UP, 2) + chunk, WIRE),
            pltpu.VMEM((UP, 2) + chunk, WIRE),
            pltpu.VMEM((DOWN, 2) + chunk, WIRE),
            pltpu.VMEM((DOWN, 2) + chunk, WIRE),
            pltpu.VMEM((DOWN, 4, PAD, LANES), BF16),
            pltpu.VMEM((UP, 4, PAD, LANES), BF16),
            pltpu.VMEM((PLANE - 1, Z, PAD, LANES), BF16),
            pltpu.VMEM((PLANE, Z, PAD, LANES), BF16),
            pltpu.VMEM((PLANE, 2, PAD, LANES), F32),
            pltpu.VMEM((PLANE, 2, PAD, LANES), F32),
            pltpu.VMEM((TENSOR, 64, 128), F32),
            pltpu.VMEM((Z * PLANE, PAD, LANES), BF16),
            dma((2,)),
            dma((2,)),
            dma((2,)),
            dma((UP, 2)),
            dma((UP, 2)),
            dma((DOWN, 2)),
            dma((DOWN, 2)),
            dma((DOWN,)),
            dma((DOWN,)),
            dma((UP,)),
            dma((UP,)),
            dma((STEPS, PLANE - 1)),
            dma((STEPS, PLANE)),
            dma((PLANE - 1,)),
            dma((PLANE,)),
            dma((TENSOR - 1,)),
            dma((TENSOR,)),
        ],
        compiler_params=pltpu.CompilerParams(
            collective_id=0,
            has_side_effects=True,
            vmem_limit_bytes=40 * 1024 * 1024,
        ),
        cost_estimate=pl.CostEstimate(
            flops=2_000_000_000, bytes_accessed=8_000_000, transcendentals=0
        ),
        name="exchange",
    )(adapters, table, inverse, tokens, down, mine, grads)


def on_device(
    tokens,
    frozen_gate_up,
    frozen_down_factor,
    prior_b_factors,
    first_moment_owned,
    second_moment_owned,
    replica_gradients,
    adapter_of_block,
    live_row_count,
    owner_block_table,
):
    my_index = lax.axis_index("dp")
    adapters, _, owned_rows, rank = prior_b_factors.shape
    width = replica_gradients.shape[3]
    inverse = owner_inverse(owner_block_table)
    mine = (
        prior_b_factors.astype(BF16)
        .transpose(0, 2, 1, 3)
        .reshape(adapters, owned_rows, 2 * rank)
    )
    mine = jnp.pad(mine, ((0, 0), (0, PAD - owned_rows), (0, 0)))
    grads = (
        replica_gradients.reshape(adapters, 2, width, rank)
        .transpose(0, 1, 3, 2)
        .reshape(adapters, 2 * rank, width)
    )
    chosen, shrunk, total = exchange(
        adapter_of_block.reshape(-1),
        owner_block_table,
        inverse,
        tokens,
        frozen_down_factor,
        mine,
        grads,
    )
    grad_total = (
        total[:, :owned_rows].reshape(adapters, owned_rows, 2, rank).transpose(0, 2, 1, 3)
    )
    adapter_change = jnp.einsum(
        "rn,crg->ncg", shrunk, chosen.reshape(2, rank, width), preferred_element_type=F32
    )
    count = lax.dynamic_index_in_dim(live_row_count, my_index, 0, keepdims=False)
    pre = frozen_gate_up.astype(F32) + ADAPTER_SCALE * adapter_change
    gated = jax.nn.silu(pre[:, 0]) * pre[:, 1]
    live = jnp.arange(tokens.shape[0], dtype=jnp.int32) < count
    hidden = jnp.where(live[:, None], gated, F32(0.0)).astype(BF16)
    new_m = BETA_ONE * first_moment_owned + (1.0 - BETA_ONE) * grad_total
    new_v = BETA_TWO * second_moment_owned + (1.0 - BETA_TWO) * grad_total * grad_total
    m_hat = new_m / (1.0 - BETA_ONE**ADAM_STEP)
    v_hat = new_v / (1.0 - BETA_TWO**ADAM_STEP)
    new_b = prior_b_factors - LEARN_RATE * m_hat / (jnp.sqrt(v_hat) + EPSILON)
    return (new_b, new_m, new_v, hidden)


def solution(mesh):
    placed = (
        P("dp", "tensor"),
        P("dp", None, "tensor"),
        P(None, None, "tensor"),
        P(None, None, ("tensor", "dp"), None),
        P(None, None, ("tensor", "dp"), None),
        P(None, None, ("tensor", "dp"), None),
        P("dp", None, None, "tensor", None),
        P(),
        P(),
        P(),
    )
    return jax.shard_map(
        on_device,
        mesh=mesh,
        in_specs=placed,
        out_specs=(
            P(None, None, ("tensor", "dp"), None),
            P(None, None, ("tensor", "dp"), None),
            P(None, None, ("tensor", "dp"), None),
            P("dp", "tensor"),
        ),
        check_vma=False,
    )
```

time: 729 us -> 70.4 us (0.10)
  waiting for transfers between devices: 599 us -> 0 us
  local copies, waits for them, and re-layouts: 72.7 us -> 8.47 us
  Pallas kernels: 0 us -> 56.8 us
  blocking collectives: 28.1 us -> 0 us
  between operations: 16.8 us -> 0.76 us
    unnamed x3 -> x0, waiting for transfers between devices: 527 us -> none
    all_gather x1 -> x0, waiting for transfers between devices: 71.8 us -> none  [on_device(): everyone = lax.all_gather(prior, 'dp', axis=2, tiled=True)]
    pallas_call x0 -> x1, Pallas kernels: none -> 56.8 us  [exchange(): pl.pallas_call(exchange_kernel, out_shape=(jax.ShapeDtypeStruct((LANES, 1...]
    psum x1 -> x0, blocking collectives: 28.1 us -> none  [on_device(): shrunk = lax.psum(partial_value, 'tensor').astype(jnp.bfloat16)]
    gather x5 -> x0, local copies, waits for them, and re-layouts: 23.3 us -> none  [the longest x2 13.6 us: on_device(): everyone.reshape(adapters, 2, n_owners, owned_rows, rank)[:, :, inverse]]
    convert_element_type x2 -> x0, local copies, waits for them, and re-layouts: 21.7 us -> none  [on_device(): ordered = parts[:, :, owner_block_table].reshape(adapters, 2, local_hidde...]
    convert_element_type x3 -> x1, other arithmetic: 8.96 us -> 1.1 us  [on_device(): hidden = jnp.where(live[:, None], gated, F32(0.0)).astype(BF16)]
  transfers between devices with their start and end apart: 2 -> 0, of which waited for: 2 -> 0; matrix products, arithmetic and copies ran while one was open for 11% -> 0% of each run, Pallas kernels for 0% -> 0%
where the time goes in v1:
time: 70.4 us; the launch traced here: 70.1 us
  Pallas kernels  56.8 us (81%)
  local copies, waits for them, and re-layouts  8.47 us (12%)
  other arithmetic  3.67 us (5%)
  between operations  0.76 us (1%)
    pallas_call x1, Pallas kernels, exchange(): pl.pallas_call(exchange_kernel, out_shape=(jax.ShapeDtypeStruct((LANES, 1...  56.8 us
    unnamed x23, local copies, waits for them, and re-layouts  7.66 us

profile of v1, /device:TPU:1, one launch (start us, length us, event | category | flops | bytes accessed | tf_op | source)
XLA Modules:
  0.0 70.1 jit_solution(6334878588954216088)
XLA Ops:
  0.6 0.0 copy-start
  0.6 0.6 copy-done
  1.3 0.6 constant_dynamic-slice_fusion
  1.9 0.6 iota_compare_fusion.1
  2.5 0.9 %convert_bitcast_fusion = bf16[4,30,2,64]{3,2,1,0:T(2,128)(2,1)S(1)} fusion(f32[4,2,30,64]{3,1,2,0:T(2,128)} %param.13), kind=kLoop, calls=%fused_computation.14 | loop fusion | flops 15360 | bytes 92160 | tf_op jit(solution)/shard_map/transpose | solution.py:462
  3.5 0.1 reshape.39
  3.6 0.8 %select_reduce_fusion.inverse_ref = s32[64]{0:T(128)S(1)} fusion(s32[64]{0:T(128)} %table_ref.1), kind=kLoop, calls=%fused_computation.15 | loop fusion | flops 12224 | bytes 512 | tf_op jit(solution)/shard_map/reduce_sum | solution.py:37
  4.4 0.0 copy-start.1
  4.4 1.5 %copy-done.1 = bf16[1,4,2,1920,64]{3,4,2,1,0:T(8,128)(2,1)S(1)} copy-done((bf16[1,4,2,1920,64]{3,4,2,1,0:T(8,128)(2,1)S(1)}, bf16[1,4,2,1920,64]{3,4,2,1,0:T(8,128)(2,1)}, u32[]{:S(2)}) %copy-start.1) | copy-done | bytes 1966104
  5.9 1.0 %copy-done.2 = bf16[4,64,1024]{2,1,0:T(8,128)(2,1)S(1)} copy-done((bf16[4,64,1024]{2,1,0:T(8,128)(2,1)S(1)}, bf16[4,64,1024]{2,1,0:T(8,128)(2,1)}, u32[]{:S(2)}) %copy-start.2) | copy-done | bytes 524312
  7.0 0.9 %copy-done.3 = bf16[128,1024]{1,0:T(8,128)(2,1)S(1)} copy-done((bf16[128,1024]{1,0:T(8,128)(2,1)S(1)}, bf16[128,1024]{1,0:T(8,128)(2,1)}, u32[]{:S(2)}) %copy-start.3) | copy-done | bytes 262168
  7.9 0.7 copy-done.4
  8.6 0.7 copy-done.5
  9.2 56.8 %exchange.1 = (bf16[128,1920]{1,0:T(8,128)(2,1)S(1)}, bf16[64,128]{1,0:T(8,128)(2,1)S(1)}, f32[4,32,128]{2,1,0:T(8,128)S(1)}) custom-call(s32[64]{0:T(128)S(1)} %bitcast.37, s32[64]{0:T(128)S(1)} %copy-done.5, s32[64]{0:T(128)S(1)} %select_reduce_fusion.inverse_ref, bf16[128,1024]{1,0:T(8,128)(2,1)S(1)} %copy-done.3, bf16[4,64,1024]{2,1,0:T(8,128)(2,1)S(1)} %copy-done.2, ...), custom_call_target="tpu_custom_call" | custom-call | flops 2000000000 | bytes 8000000 | tf_op jit(solution)/shard_map/exchange/pallas_call | solution.py:389
  66.0 0.4 fusion
  66.5 0.0 copy-start.7
  66.5 0.0 copy-start.8
  66.5 0.0 copy-start.9
  66.5 1.1 %fusion.3 = bf16[128,1920]{1,0:T(8,128)(2,1)} fusion(f32[128,2,1920]{2,0,1:T(8,128)S(1)} %fusion, pred[128]{0:T(512)(128)(4,1)S(1)} %iota_compare_fusion.1), kind=kLoop, calls=%fused_computation.5 | loop fusion | flops 1720320 | bytes 2457728 | tf_op jit(solution)/shard_map/convert_element_type | solution.py:490
  67.6 0.1 reshape.40
  67.8 0.2 copy_subtract_fusion
  68.0 0.7 %copy.43 = f32[4,2,30,64]{3,1,2,0:T(2,128)} copy(f32[4,2,30,64]{3,0,2,1:T(4,128)S(1)} %get-tuple-element.22) | data formatting | bytes 122880
  68.7 0.7 %copy.44 = f32[4,2,30,64]{3,1,2,0:T(2,128)} copy(f32[4,2,30,64]{3,0,2,1:T(4,128)S(1)} %get-tuple-element.23) | data formatting | bytes 122880
  69.4 0.7 %copy.45 = f32[4,2,30,64]{3,1,2,0:T(2,128)} copy(f32[4,2,30,64]{3,0,2,1:T(4,128)S(1)} %get-tuple-element.24) | data formatting | bytes 122880
  (10 shorter events, 0.0 us)
Async XLA Ops:
  0.6 0.7 copy-start
  4.4 1.6 %copy-start.1 = (bf16[1,4,2,1920,64]{3,4,2,1,0:T(8,128)(2,1)S(1)}, bf16[1,4,2,1920,64]{3,4,2,1,0:T(8,128)(2,1)}, u32[]{:S(2)}) copy-start(bf16[1,4,2,1920,64]{3,4,2,1,0:T(8,128)(2,1)} %param.16) | copy-start | bytes 5898244
  5.9 1.0 %copy-start.2 = (bf16[4,64,1024]{2,1,0:T(8,128)(2,1)S(1)}, bf16[4,64,1024]{2,1,0:T(8,128)(2,1)}, u32[]{:S(2)}) copy-start(bf16[4,64,1024]{2,1,0:T(8,128)(2,1)} %down_ref.1) | copy-start | bytes 1572868
  7.0 0.9 %copy-start.3 = (bf16[128,1024]{1,0:T(8,128)(2,1)S(1)}, bf16[128,1024]{1,0:T(8,128)(2,1)}, u32[]{:S(2)}) copy-start(bf16[128,1024]{1,0:T(8,128)(2,1)} %tokens_ref.1) | copy-start | bytes 786436
  7.9 0.7 copy-start.4
  8.6 0.7 copy-start.5
  9.2 56.8 %copy-start.6 = (bf16[128,2,1920]{2,1,0:T(2,128)(2,1)S(1)}, bf16[128,2,1920]{2,1,0:T(2,128)(2,1)}, u32[]{:S(2)}) copy-start(bf16[128,2,1920]{2,1,0:T(2,128)(2,1)} %param.11) | copy-start | bytes 2949124
  66.5 1.3 %copy-start.7 = (f32[4,2,30,64]{3,1,2,0:T(2,128)S(1)}, f32[4,2,30,64]{3,1,2,0:T(2,128)}, u32[]{:S(2)}) copy-start(f32[4,2,30,64]{3,1,2,0:T(2,128)} %param.13) | copy-start | bytes 184324
  66.5 1.3 %copy-start.8 = (f32[4,2,30,64]{3,1,2,0:T(2,128)S(1)}, f32[4,2,30,64]{3,1,2,0:T(2,128)}, u32[]{:S(2)}) copy-start(f32[4,2,30,64]{3,1,2,0:T(2,128)} %param.14) | copy-start | bytes 184324
  66.5 1.3 %copy-start.9 = (f32[4,2,30,64]{3,1,2,0:T(2,128)S(1)}, f32[4,2,30,64]{3,1,2,0:T(2,128)}, u32[]{:S(2)}) copy-start(f32[4,2,30,64]{3,1,2,0:T(2,128)} %param.15) | copy-start | bytes 184324

commit v2 on v1

v2 whole, which is shorter than its diff:
```python
import functools

import jax
import jax.numpy as jnp
from jax import lax
from jax.experimental import pallas as pl
from jax.experimental.pallas import tpu as pltpu
from jax.sharding import PartitionSpec as P

ADAM_STEP = 20


ADAPTER_SCALE = 2.0
BETA_ONE = 0.9
BETA_TWO = 0.95
LEARN_RATE = 0.05
EPSILON = 1e-08

MESH = pl.DeviceIdType.MESH
Z = 16
PLANE = 4
TENSOR = 8
UP = Z // 2 - 1
DOWN = Z // 2
STEPS = Z // 2
FB = 30
PAD = 32
LANES = 128
WIRE = jnp.bfloat16
VMEM_LIMIT = 60 * 1024 * 1024
F32 = jnp.float32
BF16 = jnp.bfloat16


def slots_of_batch(step):
    if step == 0:
        return 0, 3
    if step == STEPS - 1:
        return 2 * step + 1, 1
    return 2 * step + 1, 2


def exchange_kernel(
    adapters_ref,
    table_ref,
    counts_ref,
    table_row_ref,
    tokens_ref,
    down_ref,
    prior_ref,
    grads_ref,
    bt_ref,
    shrunk_ref,
    live_ref,
    total_ref,
    tokens_in,
    down_in_all,
    prior_in,
    wide,
    mine,
    inverse_row,
    inverse,
    own_half,
    other_half,
    own_terms,
    other_terms,
    core_out,
    core_in,
    staged,
    up_out,
    up_in,
    down_out,
    down_in,
    gather_up,
    gather_down,
    spread_out,
    spread_in,
    final_out,
    final_in,
    partial_sums,
    natural,
    local_sem,
    core_send,
    core_recv,
    up_send,
    up_recv,
    down_send,
    down_recv,
    gup_send,
    gup_recv,
    gdown_send,
    gdown_recv,
    spread_send,
    spread_recv,
    final_send,
    final_recv,
    psum_send,
    psum_recv,
):
    dp = lax.axis_index("dp")
    tensor = lax.axis_index("tensor")
    z = dp // PLANE
    plane = dp % PLANE
    core = plane % 2
    base = z * PLANE
    above = (lax.rem(z + 1, Z) * PLANE + plane, tensor)
    below = (lax.rem(z + Z - 1, Z) * PLANE + plane, tensor)
    sibling = (base + plane - core + (1 - core), tensor)
    mates = [lax.rem(plane + step, PLANE) for step in range(1, PLANE)]
    mate_ids = [(base + mate, tensor) for mate in mates]
    peers = [lax.rem(tensor + step, TENSOR) for step in range(1, TENSOR)]
    peer_ids = [(dp, peer) for peer in peers]

    barrier = pltpu.get_barrier_semaphore()
    everyone = [above, below] + mate_ids + peer_ids
    for device in everyone:
        pl.semaphore_signal(barrier, inc=1, device_id=device, device_id_type=MESH)

    def local(src, dst, i):
        copy = pltpu.make_async_copy(src, dst, local_sem.at[i])
        copy.start()
        return copy

    get_prior = local(prior_ref, prior_in, 0)
    get_other = local(grads_ref.at[pl.ds(2 * (1 - core), 2)], other_half, 1)
    get_own = local(grads_ref.at[pl.ds(2 * core, 2)], own_half, 2)
    get_down = local(down_ref, down_in_all, 3)
    get_tokens = local(tokens_ref, tokens_in, 4)

    wide[...] = jnp.zeros_like(wide)
    row = lax.broadcasted_iota(jnp.int32, (64, 64), 0)
    column = lax.broadcasted_iota(jnp.int32, (64, 64), 1)
    table_rows = jnp.broadcast_to(table_row_ref[...], (64, 64))
    table_column = jnp.sum(jnp.where(row == column, table_rows, 0), axis=1, keepdims=True)
    inverse_row[...] = jnp.sum(jnp.where(table_column == column, row, 0), axis=0, keepdims=True)
    get_inverse = local(inverse_row, inverse, 5)

    get_prior.wait()
    for a in range(4):
        for c in range(2):
            wide[a, pl.ds(0, FB), pl.ds(64 * c, 64)] = prior_in[
                pl.ds(2 * FB * a + c, FB, stride=2), :
            ]
    mine[...] = wide[...].astype(BF16)

    def picker(q):
        window = jnp.minimum((120 * q) // LANES * LANES, 1920 - 2 * LANES)
        offset = 120 * q - window
        row = lax.broadcasted_iota(jnp.int32, (PLANE * PAD, 2 * LANES), 0)
        column = lax.broadcasted_iota(jnp.int32, (PLANE * PAD, 2 * LANES), 1)
        hit = (column == offset + row - 2 * (row // PAD)) & (row % PAD < FB)
        return pl.multiple_of(window, LANES), jnp.where(hit, F32(1.0), F32(0.0)).astype(BF16)

    def turn(half, terms):
        @pl.loop(0, Z, unroll=2)
        def _(q):
            window, pick = picker(q)
            for p in range(2):
                block = lax.dot_general(
                    pick,
                    half[p, :, pl.ds(window, 2 * LANES)],
                    (((1,), (1,)), ((), ())),
                    preferred_element_type=F32,
                )
                terms[pl.ds(PLANE * q, PLANE), p] = block.reshape(PLANE, PAD, LANES).astype(BF16)

    get_other.wait()
    turn(other_half, other_terms)

    pl.semaphore_wait(barrier, len(everyone))

    def remote(src, dst, send, recv, device):
        return pltpu.make_async_remote_copy(
            src_ref=src,
            dst_ref=dst,
            send_sem=send,
            recv_sem=recv,
            device_id=device,
            device_id_type=MESH,
        )

    def go_up(step):
        source = mine if step == 0 else gather_up.at[step - 1]
        return remote(source, gather_up.at[step], gup_send.at[step], gup_recv.at[step], above)

    def go_down(step):
        source = mine if step == 0 else gather_down.at[step - 1]
        return remote(source, gather_down.at[step], gdown_send.at[step], gdown_recv.at[step], below)

    gups = [go_up(step) for step in range(DOWN)]
    gdowns = [go_down(step) for step in range(UP)]
    gups[0].start()
    gdowns[0].start()

    def target_of(way, step):
        if way == 0:
            return lax.rem(z + UP - step, Z)
        return lax.rem(z + Z - DOWN + step, Z)

    def chunk_of(way, step):
        return 2 * step + way

    core_copies = [
        remote(core_out.at[n], core_in.at[n], core_send.at[n], core_recv.at[n], sibling)
        for n in range(2 * STEPS)
    ]

    def serve(step):
        for way in range(2):
            n = chunk_of(way, step)
            target = z if way == 0 and step == UP else target_of(way, step)
            for b in range(PLANE):
                core_out[n, :, b] = other_terms[table_ref[PLANE * target + b]]
            core_copies[n].start()

    serve(0)
    serve(1)

    get_own.wait()
    turn(own_half, own_terms)

    get_down.wait()
    get_tokens.wait()
    partial_sums[tensor] = lax.dot_general(
        down_in_all[adapters_ref[dp]],
        tokens_in[...],
        (((1,), (1,)), ((), ())),
        preferred_element_type=F32,
    )
    psums = [
        remote(
            partial_sums.at[tensor],
            partial_sums.at[tensor],
            psum_send.at[i],
            psum_recv.at[tensor],
            device,
        )
        for i, device in enumerate(peer_ids)
    ]
    for copy in psums:
        copy.start()
    plane_adapters = [adapters_ref[base + lax.rem(plane + step, PLANE)] for step in range(PLANE)]
    live_ref[...] = (
        lax.broadcasted_iota(jnp.int32, (1, 128), 1) < counts_ref[dp]
    ).astype(jnp.int32)

    def send(way, step, p):
        out, into, send_sem, recv_sem = (
            (up_out, up_in, up_send, up_recv)
            if way == 0
            else (down_out, down_in, down_send, down_recv)
        )
        return remote(
            out.at[step, p],
            into.at[step, p],
            send_sem.at[step, p],
            recv_sem.at[step, p],
            above if way == 0 else below,
        )

    hops = [
        [[send(way, step, p) for p in range(2)] for step in range((UP, DOWN)[way])]
        for way in range(2)
    ]

    def prepare(step):
        for way in range(2):
            n = chunk_of(way, step)
            target = z if way == 0 and step == UP else target_of(way, step)
            core_copies[n].wait_recv()
            for b in range(PLANE):
                staged[way, :, b] = own_terms[table_ref[PLANE * target + b]].astype(F32) + core_in[
                    n, :, b
                ].astype(F32)

    def spread(step, i):
        first, count = slots_of_batch(step)
        return remote(
            spread_out.at[i, pl.ds(first, count)],
            spread_in.at[plane, pl.ds(first, count)],
            spread_send.at[step, i],
            spread_recv.at[step, plane],
            mate_ids[i],
        )

    def choose(block, adapter):
        result = block[0]
        for a in range(1, 4):
            result = jnp.where(adapter == a, block[a], result)
        return result

    spreads = []

    def gather(step):
        arrived = []
        if step == 0:
            arrived.append(mine[...])
        gups[step].wait_recv()
        if step + 1 < DOWN:
            gups[step + 1].start()
        arrived.append(gather_up[step])
        if step < UP:
            gdowns[step].wait_recv()
            if step + 1 < UP:
                gdowns[step + 1].start()
            arrived.append(gather_down[step])
        first, count = slots_of_batch(step)
        for n in range(count):
            spread_in[plane, first + n] = choose(arrived[n], plane_adapters[0])
            for i in range(PLANE - 1):
                spread_out[i, first + n] = choose(arrived[n], plane_adapters[i + 1])
        for i in range(PLANE - 1):
            copy = spread(step, i)
            copy.start()
            spreads.append(copy)

    prepare(0)
    for step in range(STEPS):
        for p in range(2):
            for way in range(2):
                if way == 0 and step == UP:
                    continue
                value = staged[way, p]
                if step > 0:
                    hops[way][step - 1][p].wait_recv()
                    value = value + (up_in, down_in)[way][step - 1, p].astype(F32)
                (up_out, down_out)[way][step, p] = value.astype(WIRE)
                hops[way][step][p].start()
        if step + 2 < STEPS:
            serve(step + 2)
        gather(step)
        if step + 1 < STEPS:
            prepare(step + 1)

    for p in range(2):
        hops[0][UP - 1][p].wait_recv()
        hops[1][DOWN - 1][p].wait_recv()
        final_out[:, p] = (
            staged[0, p] + up_in[UP - 1, p].astype(F32) + down_in[DOWN - 1, p].astype(F32)
        )
    finals = [
        remote(
            final_out.at[mate],
            final_in.at[plane],
            final_send.at[i],
            final_recv.at[plane],
            mate_ids[i],
        )
        for i, mate in enumerate(mates)
    ]
    for copy in finals:
        copy.start()
    final_in[plane] = final_out[plane]

    for peer in peers:
        remote(
            partial_sums.at[peer],
            partial_sums.at[peer],
            psum_send.at[0],
            psum_recv.at[peer],
            peer_ids[0],
        ).wait_recv()
    shrunk = partial_sums[0]
    for i in range(1, TENSOR):
        shrunk = shrunk + partial_sums[i]
    shrunk_ref[...] = shrunk.astype(BF16)

    for step in range(STEPS):
        first, count = slots_of_batch(step)
        for i, mate in enumerate(mates):
            remote(
                spread_out.at[i, pl.ds(first, count)],
                spread_in.at[mate, pl.ds(first, count)],
                spread_send.at[step, i],
                spread_recv.at[step, mate],
                mate_ids[i],
            ).wait_recv()

    get_inverse.wait()

    @pl.loop(0, Z * PLANE, unroll=8)
    def _(k):
        owner = inverse[0, k]
        delta = lax.rem(owner // PLANE - z + Z, Z)
        slot = jnp.where(delta < STEPS, 2 * delta, 2 * Z - 1 - 2 * delta)
        natural[k] = spread_in[owner % PLANE, slot]

    @pl.loop(0, 1920 // LANES, unroll=5)
    def _(t):
        first = jnp.minimum((LANES * t) // FB, Z * PLANE - 6)
        offset = LANES * t - FB * first
        row = lax.broadcasted_iota(jnp.int32, (6 * PAD, LANES), 0)
        column = lax.broadcasted_iota(jnp.int32, (6 * PAD, LANES), 1)
        hit = (row - 2 * (row // PAD) == offset + column) & (row % PAD < FB)
        pick = jnp.where(hit, F32(1.0), F32(0.0)).astype(BF16)
        block = lax.dot_general(
            natural[pl.ds(first, 6)].reshape(6 * PAD, LANES),
            pick,
            (((0,), (0,)), ((), ())),
            preferred_element_type=F32,
        )
        bt_ref[:, pl.ds(pl.multiple_of(t * LANES, LANES), LANES)] = block.astype(BF16)

    for i, mate in enumerate(mates):
        remote(
            final_out.at[mate],
            final_in.at[mate],
            final_send.at[i],
            final_recv.at[mate],
            mate_ids[i],
        ).wait_recv()
    for c in range(2):
        for p in range(2):
            total_ref[2 * c + p] = final_in[c, p] + final_in[2 + c, p]

    for copy in core_copies + gups + gdowns + psums + spreads + finals:
        copy.wait_send()
    for way in hops:
        for pair in way:
            for copy in pair:
                copy.wait_send()


def exchange(adapters, table, counts, tokens, down, prior, grads):
    smem = pl.BlockSpec(memory_space=pltpu.SMEM)
    vmem = pl.BlockSpec(memory_space=pltpu.VMEM)
    hbm = pl.BlockSpec(memory_space=pl.ANY)
    dma = pltpu.SemaphoreType.DMA
    chunk = (PLANE, PAD, LANES)
    return pl.pallas_call(
        exchange_kernel,
        out_shape=(
            jax.ShapeDtypeStruct((LANES, 1920), BF16),
            jax.ShapeDtypeStruct((64, 128), BF16),
            jax.ShapeDtypeStruct((1, 128), jnp.int32),
            jax.ShapeDtypeStruct((4, PAD, LANES), F32),
        ),
        in_specs=[smem, smem, smem, vmem, hbm, hbm, hbm, hbm],
        out_specs=(vmem, vmem, vmem, vmem),
        scratch_shapes=[
            pltpu.VMEM((128, 1024), BF16),
            pltpu.VMEM((4, 64, 1024), BF16),
            pltpu.VMEM((240, 64), F32),
            pltpu.VMEM((4, PAD, LANES), F32),
            pltpu.VMEM((4, PAD, LANES), BF16),
            pltpu.VMEM((1, 64), jnp.int32),
            pltpu.SMEM((1, 64), jnp.int32),
            pltpu.VMEM((2, LANES, 1920), BF16),
            pltpu.VMEM((2, LANES, 1920), BF16),
            pltpu.VMEM((Z * PLANE, 2, PAD, LANES), BF16),
            pltpu.VMEM((Z * PLANE, 2, PAD, LANES), BF16),
            pltpu.VMEM((2 * STEPS, 2) + chunk, BF16),
            pltpu.VMEM((2 * STEPS, 2) + chunk, BF16),
            pltpu.VMEM((2, 2) + chunk, F32),
            pltpu.VMEM((UP, 2) + chunk, WIRE),
            pltpu.VMEM((UP, 2) + chunk, WIRE),
            pltpu.VMEM((DOWN, 2) + chunk, WIRE),
            pltpu.VMEM((DOWN, 2) + chunk, WIRE),
            pltpu.VMEM((DOWN, 4, PAD, LANES), BF16),
            pltpu.VMEM((UP, 4, PAD, LANES), BF16),
            pltpu.VMEM((PLANE - 1, Z, PAD, LANES), BF16),
            pltpu.VMEM((PLANE, Z, PAD, LANES), BF16),
            pltpu.VMEM((PLANE, 2, PAD, LANES), F32),
            pltpu.VMEM((PLANE, 2, PAD, LANES), F32),
            pltpu.VMEM((TENSOR, 64, 128), F32),
            pltpu.VMEM((Z * PLANE, PAD, LANES), BF16),
            dma((6,)),
            dma((2 * STEPS,)),
            dma((2 * STEPS,)),
            dma((UP, 2)),
            dma((UP, 2)),
            dma((DOWN, 2)),
            dma((DOWN, 2)),
            dma((DOWN,)),
            dma((DOWN,)),
            dma((UP,)),
            dma((UP,)),
            dma((STEPS, PLANE - 1)),
            dma((STEPS, PLANE)),
            dma((PLANE - 1,)),
            dma((PLANE,)),
            dma((TENSOR - 1,)),
            dma((TENSOR,)),
        ],
        compiler_params=pltpu.CompilerParams(
            collective_id=0,
            has_side_effects=True,
            vmem_limit_bytes=VMEM_LIMIT,
        ),
        cost_estimate=pl.CostEstimate(
            flops=2_000_000_000, bytes_accessed=8_000_000, transcendentals=0
        ),
        name="exchange",
    )(adapters, table, counts, table.reshape(1, -1), tokens, down, prior, grads)


def adam_kernel(total_ref, prior_ref, first_ref, second_ref, b_ref, m_ref, v_ref):
    for a in range(4):
        for c in range(2):
            grad = total_ref[a, pl.ds(0, FB), pl.ds(64 * c, 64)]
            rows = pl.ds(2 * FB * a + c, FB, stride=2)
            new_m = BETA_ONE * first_ref[rows, :] + (1.0 - BETA_ONE) * grad
            new_v = BETA_TWO * second_ref[rows, :] + (1.0 - BETA_TWO) * grad * grad
            m_hat = new_m / (1.0 - BETA_ONE**ADAM_STEP)
            v_hat = new_v / (1.0 - BETA_TWO**ADAM_STEP)
            b_ref[rows, :] = prior_ref[rows, :] - LEARN_RATE * m_hat / (jnp.sqrt(v_hat) + EPSILON)
            m_ref[rows, :] = new_m
            v_ref[rows, :] = new_v


def adam(total, prior, first, second):
    vmem = pl.BlockSpec(memory_space=pltpu.VMEM)
    return pl.pallas_call(
        adam_kernel,
        out_shape=(jax.ShapeDtypeStruct((240, 64), F32),) * 3,
        in_specs=[vmem] * 4,
        out_specs=(vmem,) * 3,
        name="adam",
    )(total, prior, first, second)


def on_device(
    tokens,
    frozen_gate_up,
    frozen_down_factor,
    prior_b_factors,
    first_moment_owned,
    second_moment_owned,
    replica_gradients,
    adapter_of_block,
    live_row_count,
    owner_block_table,
):
    adapters, _, owned_rows, rank = prior_b_factors.shape
    width = replica_gradients.shape[3]

    def flat(array):
        return array.transpose(0, 2, 1, 3).reshape(adapters * owned_rows * 2, rank)

    def shaped(array):
        return array.reshape(adapters, owned_rows, 2, rank).transpose(0, 2, 1, 3)

    prior = flat(prior_b_factors)
    grads = (
        replica_gradients.reshape(adapters, 2, width, rank)
        .transpose(0, 1, 3, 2)
        .reshape(adapters, 2 * rank, width)
    )
    chosen, shrunk, live, total = exchange(
        adapter_of_block.reshape(-1),
        owner_block_table,
        live_row_count.reshape(-1),
        tokens,
        frozen_down_factor,
        prior,
        grads,
    )
    adapter_change = jnp.einsum(
        "rn,crg->ncg", shrunk, chosen.reshape(2, rank, width), preferred_element_type=F32
    )
    pre = frozen_gate_up.astype(F32) + ADAPTER_SCALE * adapter_change
    gated = jax.nn.silu(pre[:, 0]) * pre[:, 1]
    hidden = jnp.where((live[0] > 0)[:, None], gated, F32(0.0)).astype(BF16)
    new_b, new_m, new_v = adam(total, prior, flat(first_moment_owned), flat(second_moment_owned))
    return (shaped(new_b), shaped(new_m), shaped(new_v), hidden)


def solution(mesh):
    placed = (
        P("dp", "tensor"),
        P("dp", None, "tensor"),
        P(None, None, "tensor"),
        P(None, None, ("tensor", "dp"), None),
        P(None, None, ("tensor", "dp"), None),
        P(None, None, ("tensor", "dp"), None),
        P("dp", None, None, "tensor", None),
        P(),
        P(),
        P(),
    )
    return jax.shard_map(
        on_device,
        mesh=mesh,
        in_specs=placed,
        out_specs=(
            P(None, None, ("tensor", "dp"), None),
            P(None, None, ("tensor", "dp"), None),
            P(None, None, ("tensor", "dp"), None),
            P("dp", "tensor"),
        ),
        check_vma=False,
    )
```

time: 70.4 us -> 56.2 us (0.80)
  local copies, waits for them, and re-layouts: 8.47 us -> 0.01 us
  Pallas kernels: 56.8 us -> 52.7 us
  other arithmetic: 3.67 us -> 1.1 us
  matrix products: 0.44 us -> 1.49 us
    unnamed x23 -> x4, local copies, waits for them, and re-layouts: 7.66 us -> 0.01 us
    pallas_call x1, Pallas kernels: 56.8 us -> 50.8 us  [exchange(): pl.pallas_call(exchange_kernel, out_shape=(jax.ShapeDtypeStruct((LANES, 1...]
    pallas_call x0 -> x1, Pallas kernels: none -> 1.9 us  [adam(): pl.pallas_call(adam_kernel, out_shape=(jax.ShapeDtypeStruct((240, 64), F3...]
    dot_general x1, matrix products: 0.44 us -> 1.49 us  [on_device(): jnp.einsum('rn,crg->ncg', shrunk, chosen.reshape(2, rank, width), preferr...]
    transpose x1 -> x0, other arithmetic: 0.95 us -> none  [on_device(): mine = prior_b_factors.astype(BF16).transpose(0, 2, 1, 3).reshape(adapter...]
    reduce_sum x1 -> x0, other arithmetic: 0.76 us -> none  [owner_inverse(): jnp.sum(jnp.where(owner_block_table[None, :] == iota[:, None], iota[None,...]
where the time goes in v2:
time: 56.2 us; the launch traced here: 56 us
  Pallas kernels  52.7 us (94%)
  matrix products  1.49 us (3%)
  other arithmetic  1.1 us (2%)
  between operations  0.69 us (1%)
    pallas_call x1, Pallas kernels, exchange(): pl.pallas_call(exchange_kernel, out_shape=(jax.ShapeDtypeStruct((LANES, 1...  50.8 us
    pallas_call x1, Pallas kernels, adam(): pl.pallas_call(adam_kernel, out_shape=(jax.ShapeDtypeStruct((240, 64), F3...  1.9 us
    dot_general x1, matrix products, on_device(): jnp.einsum('rn,crg->ncg', shrunk, chosen.reshape(2, rank, width), preferr...  1.49 us

profile of v2, /device:TPU:1, one launch (start us, length us, event | category | flops | bytes accessed | tf_op | source)
XLA Modules:
  0.0 56.0 jit_solution(6635732641876750257)
XLA Ops:
  0.6 0.0 copy-start
  0.6 50.8 %exchange.1 = (bf16[128,1920]{1,0:T(8,128)(2,1)}, bf16[64,128]{1,0:T(8,128)(2,1)}, s32[1,128]{1,0:T(1,128)}, f32[4,32,128]{2,1,0:T(8,128)}) custom-call(s32[64]{0:T(128)} %bitcast.54, s32[64]{0:T(128)} %table_ref.1, s32[64]{0:T(128)} %bitcast.56, s32[1,64]{1,0:T(1,128)} %bitcast.55, bf16[128,1024]{1,0:T(8,128)(2,1)} %tokens_ref.1, ...), custom_call_target="tpu_custom_call" | custom-call | flops 2000000000 | bytes 8000000 | tf_op jit(solution)/shard_map/exchange/pallas_call | solution.py:430
  51.5 0.0 copy-start.1
  51.5 0.0 copy-done
  51.5 1.5 %fusion = f32[128,2,1920]{2,0,1:T(8,128)S(1)} fusion(bf16[2,64,1920]{2,1,0:T(8,128)(2,1)} %bitcast.45, bf16[128,2,1920]{2,1,0:T(2,128)(2,1)S(1)} %copy-done, bf16[64,128]{1,0:T(8,128)(2,1)} %get-tuple-element.16), kind=kOutput, calls=%fused_computation.1 | convolution fusion | flops 64389120 | bytes 3457024 | tf_op jit(solution)/shard_map/rn,crg->ncg/dot_general | solution.py:558
  53.0 0.0 copy-done.1
  53.0 1.1 %fusion.3 = bf16[128,1920]{1,0:T(8,128)(2,1)} fusion(f32[128,2,1920]{2,0,1:T(8,128)S(1)} %fusion, pred[128]{0:T(512)(128)(4,1)S(1)} %compare_bitcast_fusion), kind=kLoop, calls=%fused_computation.5 | loop fusion | flops 1720320 | bytes 2457728 | tf_op jit(solution)/shard_map/convert_element_type | solution.py:563
  54.1 1.9 %adam.1 = (f32[240,64]{1,0:T(8,128)}, f32[240,64]{1,0:T(8,128)}, f32[240,64]{1,0:T(8,128)}) custom-call(f32[4,32,128]{2,1,0:T(8,128)} %get-tuple-element.11.total_ref, f32[240,64]{1,0:T(8,128)} %bitcast.47, f32[240,64]{1,0:T(8,128)} %bitcast.48, f32[240,64]{1,0:T(8,128)} %bitcast.49), custom_call_target="tpu_custom_call" | custom-call | tf_op jit(solution)/shard_map/adam/pallas_call | solution.py:513
  (1 shorter events, 0.0 us)
Async XLA Ops:
  0.6 50.8 %copy-start = (bf16[128,2,1920]{2,1,0:T(2,128)(2,1)S(1)}, bf16[128,2,1920]{2,1,0:T(2,128)(2,1)}, u32[]{:S(2)}) copy-start(bf16[128,2,1920]{2,1,0:T(2,128)(2,1)} %param.11) | copy-start | bytes 2949124
  51.5 1.5 %copy-start.1 = (s32[1,128]{1,0:T(1,128)S(1)}, s32[1,128]{1,0:T(1,128)}, u32[]{:S(2)}) copy-start(s32[1,128]{1,0:T(1,128)} %get-tuple-element.15) | copy-start | bytes 1540

commit v3 on v2

--- a/solution.py
+++ b/solution.py
@@ -20,9 +20,9 @@
 Z = 16
 PLANE = 4
 TENSOR = 8
-UP = Z // 2 - 1
 DOWN = Z // 2
 STEPS = Z // 2
+ROUNDS = Z // 4
 FB = 30
 PAD = 32
 LANES = 128
@@ -32,19 +32,14 @@
 BF16 = jnp.bfloat16
 
 
-def slots_of_batch(step):
-    if step == 0:
-        return 0, 3
-    if step == STEPS - 1:
-        return 2 * step + 1, 1
-    return 2 * step + 1, 2
+def slots_of_batch(batch):
+    return (0, 5) if batch == 0 else (4 * batch + 1, 4 if batch < ROUNDS - 1 else 3)
 
 
 def exchange_kernel(
-    adapters_ref,
-    table_ref,
-    counts_ref,
-    table_row_ref,
+    adapters_hbm,
+    table_hbm,
+    counts_hbm,
     tokens_ref,
     down_ref,
     prior_ref,
@@ -53,6 +48,10 @@
     shrunk_ref,
     live_ref,
     total_ref,
+    adapters_ref,
+    table_ref,
+    counts_ref,
+    table_row_ref,
     tokens_in,
     down_in_all,
     prior_in,
@@ -66,13 +65,11 @@
     other_terms,
     core_out,
     core_in,
-    staged,
-    up_out,
-    up_in,
-    down_out,
-    down_in,
-    gather_up,
-    gather_down,
+    y_out,
+    y_in,
+    hop_out,
+    hop_in,
+    gathered,
     spread_out,
     spread_in,
     final_out,
@@ -82,14 +79,12 @@
     local_sem,
     core_send,
     core_recv,
-    up_send,
-    up_recv,
-    down_send,
-    down_recv,
-    gup_send,
-    gup_recv,
-    gdown_send,
-    gdown_recv,
+    y_send,
+    y_recv,
+    hop_send,
+    hop_recv,
+    gather_send,
+    gather_recv,
     spread_send,
     spread_recv,
     final_send,
@@ -102,17 +97,22 @@
     z = dp // PLANE
     plane = dp % PLANE
     core = plane % 2
+    half = plane // 2
     base = z * PLANE
-    above = (lax.rem(z + 1, Z) * PLANE + plane, tensor)
-    below = (lax.rem(z + Z - 1, Z) * PLANE + plane, tensor)
+
+    def along(distance):
+        return (lax.rem(z + Z + distance, Z) * PLANE + plane, tensor)
+
+    above, below = along(1), along(-1)
     sibling = (base + plane - core + (1 - core), tensor)
+    across = (base + (1 - half) * 2 + core, tensor)
     mates = [lax.rem(plane + step, PLANE) for step in range(1, PLANE)]
     mate_ids = [(base + mate, tensor) for mate in mates]
     peers = [lax.rem(tensor + step, TENSOR) for step in range(1, TENSOR)]
     peer_ids = [(dp, peer) for peer in peers]
 
     barrier = pltpu.get_barrier_semaphore()
-    everyone = [above, below] + mate_ids + peer_ids
+    everyone = [above, below, along(2), along(-2)] + mate_ids + peer_ids
     for device in everyone:
         pl.semaphore_signal(barrier, inc=1, device_id=device, device_id_type=MESH)
 
@@ -121,6 +121,12 @@
         copy.start()
         return copy
 
+    get_small = [
+        local(adapters_hbm, adapters_ref, 6),
+        local(table_hbm, table_ref, 7),
+        local(counts_hbm, counts_ref, 8),
+        local(table_hbm, table_row_ref, 9),
+    ]
     get_prior = local(prior_ref, prior_in, 0)
     get_other = local(grads_ref.at[pl.ds(2 * (1 - core), 2)], other_half, 1)
     get_own = local(grads_ref.at[pl.ds(2 * core, 2)], own_half, 2)
@@ -128,9 +134,11 @@
     get_tokens = local(tokens_ref, tokens_in, 4)
 
     wide[...] = jnp.zeros_like(wide)
+    for copy in get_small:
+        copy.wait()
     row = lax.broadcasted_iota(jnp.int32, (64, 64), 0)
     column = lax.broadcasted_iota(jnp.int32, (64, 64), 1)
-    table_rows = jnp.broadcast_to(table_row_ref[...], (64, 64))
+    table_rows = jnp.broadcast_to(table_row_ref[...].reshape(1, 64), (64, 64))
     table_column = jnp.sum(jnp.where(row == column, table_rows, 0), axis=1, keepdims=True)
     inverse_row[...] = jnp.sum(jnp.where(table_column == column, row, 0), axis=0, keepdims=True)
     get_inverse = local(inverse_row, inverse, 5)
@@ -179,45 +187,79 @@
             device_id_type=MESH,
         )
 
-    def go_up(step):
-        source = mine if step == 0 else gather_up.at[step - 1]
-        return remote(source, gather_up.at[step], gup_send.at[step], gup_recv.at[step], above)
-
-    def go_down(step):
-        source = mine if step == 0 else gather_down.at[step - 1]
-        return remote(source, gather_down.at[step], gdown_send.at[step], gdown_recv.at[step], below)
-
-    gups = [go_up(step) for step in range(DOWN)]
-    gdowns = [go_down(step) for step in range(UP)]
-    gups[0].start()
-    gdowns[0].start()
-
-    def target_of(way, step):
-        if way == 0:
-            return lax.rem(z + UP - step, Z)
-        return lax.rem(z + Z - DOWN + step, Z)
-
-    def chunk_of(way, step):
-        return 2 * step + way
-
+    def pass_on(way, r):
+        even = r - 1 if r % 2 else r - 2
+        return remote(
+            gathered.at[way, even - 1] if even else mine,
+            gathered.at[way, r - 1],
+            gather_send.at[way, r - 1],
+            gather_recv.at[way, r - 1],
+            along((1 if way == 0 else -1) * (r - even)),
+        )
+
+    blocks = {
+        (way, r): pass_on(way, r)
+        for r in range(1, Z // 2 + 1)
+        for way in range(2)
+        if (way, r) != (1, Z // 2)
+    }
+
+    def pass_round(batch):
+        for r in (2 * batch + 2, 2 * batch + 1):
+            for way in range(2):
+                if (way, r) in blocks:
+                    blocks[way, r].start()
+
+    pass_round(0)
+
+    def chunk_of(way, distance):
+        return 2 * (Z // 2 - distance) + way if distance else 0
+
+    def owners_of(way, distance):
+        return PLANE * lax.rem(z + Z + (distance if way == 0 else -distance), Z)
+
+    groups = [
+        [(way, r) for r in (Z // 2 - 2 * k, Z // 2 - 1 - 2 * k) for way in range(2) if (way, r) != (0, Z // 2)]
+        for k in range(Z // 4)
+    ] + [[(0, 0)]]
     core_copies = [
         remote(core_out.at[n], core_in.at[n], core_send.at[n], core_recv.at[n], sibling)
-        for n in range(2 * STEPS)
+        for n in range(Z)
     ]
-
-    def serve(step):
-        for way in range(2):
-            n = chunk_of(way, step)
-            target = z if way == 0 and step == UP else target_of(way, step)
+    y_copies = [
+        remote(y_out.at[n], y_in.at[n], y_send.at[n], y_recv.at[n], across) for n in range(Z)
+    ]
+
+    def serve(group):
+        for way, r in groups[group]:
+            n, first = chunk_of(way, r), owners_of(way, r)
             for b in range(PLANE):
-                core_out[n, :, b] = other_terms[table_ref[PLANE * target + b]]
+                core_out[n, :, b] = other_terms[table_ref[first + b]]
             core_copies[n].start()
+
+    def chip_sum(way, r, side):
+        n, first = chunk_of(way, r), owners_of(way, r) + 2 * side
+        return [
+            own_terms[table_ref[first + b]].astype(F32) + core_in[n, :, 2 * side + b].astype(F32)
+            for b in range(2)
+        ]
+
+    def serve_across(group):
+        for way, r in groups[group]:
+            n = chunk_of(way, r)
+            core_copies[n].wait_recv()
+            for b, value in enumerate(chip_sum(way, r, 1 - half)):
+                y_out[n, :, b] = value.astype(WIRE)
+            y_copies[n].start()
 
     serve(0)
     serve(1)
 
     get_own.wait()
     turn(own_half, own_terms)
+    serve_across(0)
+    serve(2)
+    serve_across(1)
 
     get_down.wait()
     get_tokens.wait()
@@ -244,43 +286,50 @@
         lax.broadcasted_iota(jnp.int32, (1, 128), 1) < counts_ref[dp]
     ).astype(jnp.int32)
 
-    def send(way, step, p):
-        out, into, send_sem, recv_sem = (
-            (up_out, up_in, up_send, up_recv)
-            if way == 0
-            else (down_out, down_in, down_send, down_recv)
+    hops = {
+        (way, r): remote(
+            hop_out.at[way, r - 1],
+            hop_in.at[way, r - 1],
+            hop_send.at[way, r - 1],
+            hop_recv.at[way, r - 1],
+            along((1 if way == 0 else -1) * (1 if r % 2 else 2)),
         )
-        return remote(
-            out.at[step, p],
-            into.at[step, p],
-            send_sem.at[step, p],
-            recv_sem.at[step, p],
-            above if way == 0 else below,
-        )
-
-    hops = [
-        [[send(way, step, p) for p in range(2)] for step in range((UP, DOWN)[way])]
-        for way in range(2)
-    ]
-
-    def prepare(step):
-        for way in range(2):
-            n = chunk_of(way, step)
-            target = z if way == 0 and step == UP else target_of(way, step)
-            core_copies[n].wait_recv()
-            for b in range(PLANE):
-                staged[way, :, b] = own_terms[table_ref[PLANE * target + b]].astype(F32) + core_in[
-                    n, :, b
-                ].astype(F32)
-
-    def spread(step, i):
-        first, count = slots_of_batch(step)
+        for group in groups[:-1]
+        for way, r in group
+    }
+
+    def plane_sum(way, r):
+        n = chunk_of(way, r)
+        y_copies[n].wait_recv()
+        return [value + y_in[n, :, b].astype(F32) for b, value in enumerate(chip_sum(way, r, half))]
+
+    def arrived_sum(way, r, values):
+        for child in (r + 1, r + 2):
+            if (way, child) in hops:
+                hops[way, child].wait_recv()
+                values = [
+                    value + hop_in[way, child - 1, :, b].astype(F32)
+                    for b, value in enumerate(values)
+                ]
+        return values
+
+    def send_round(group):
+        for way, r in groups[group]:
+            values = plane_sum(way, r)
+            if r % 2 == 0:
+                values = arrived_sum(way, r, values)
+            for b, value in enumerate(values):
+                hop_out[way, r - 1, :, b] = value.astype(WIRE)
+            hops[way, r].start()
+
+    def spread(batch, i, source, mate):
+        first, count = slots_of_batch(batch)
         return remote(
             spread_out.at[i, pl.ds(first, count)],
-            spread_in.at[plane, pl.ds(first, count)],
-            spread_send.at[step, i],
-            spread_recv.at[step, plane],
-            mate_ids[i],
+            spread_in.at[source, pl.ds(first, count)],
+            spread_send.at[batch, i],
+            spread_recv.at[batch, source],
+            mate,
         )
 
     def choose(block, adapter):
@@ -291,66 +340,53 @@
 
     spreads = []
 
-    def gather(step):
-        arrived = []
-        if step == 0:
-            arrived.append(mine[...])
-        gups[step].wait_recv()
-        if step + 1 < DOWN:
-            gups[step + 1].start()
-        arrived.append(gather_up[step])
-        if step < UP:
-            gdowns[step].wait_recv()
-            if step + 1 < UP:
-                gdowns[step + 1].start()
-            arrived.append(gather_down[step])
-        first, count = slots_of_batch(step)
-        for n in range(count):
-            spread_in[plane, first + n] = choose(arrived[n], plane_adapters[0])
-            for i in range(PLANE - 1):
-                spread_out[i, first + n] = choose(arrived[n], plane_adapters[i + 1])
+    def place(block, slot):
+        spread_in[plane, slot] = choose(block, plane_adapters[0])
         for i in range(PLANE - 1):
-            copy = spread(step, i)
+            spread_out[i, slot] = choose(block, plane_adapters[i + 1])
+
+    def gather(batch):
+        for way in range(2):
+            if (way, 2 * batch + 2) in blocks:
+                blocks[way, 2 * batch + 2].wait_recv()
+        if batch + 1 < ROUNDS:
+            pass_round(batch + 1)
+        if batch == 0:
+            place(mine[...], 0)
+        for r in (2 * batch + 1, 2 * batch + 2):
+            for way in range(2):
+                if (way, r) in blocks:
+                    if r % 2:
+                        blocks[way, r].wait_recv()
+                    place(gathered[way, r - 1], 2 * r - 1 + way)
+        for i in range(PLANE - 1):
+            copy = spread(batch, i, plane, mate_ids[i])
             copy.start()
             spreads.append(copy)
 
-    prepare(0)
-    for step in range(STEPS):
-        for p in range(2):
-            for way in range(2):
-                if way == 0 and step == UP:
-                    continue
-                value = staged[way, p]
-                if step > 0:
-                    hops[way][step - 1][p].wait_recv()
-                    value = value + (up_in, down_in)[way][step - 1, p].astype(F32)
-                (up_out, down_out)[way][step, p] = value.astype(WIRE)
-                hops[way][step][p].start()
-        if step + 2 < STEPS:
-            serve(step + 2)
-        gather(step)
-        if step + 1 < STEPS:
-            prepare(step + 1)
-
-    for p in range(2):
-        hops[0][UP - 1][p].wait_recv()
-        hops[1][DOWN - 1][p].wait_recv()
-        final_out[:, p] = (
-            staged[0, p] + up_in[UP - 1, p].astype(F32) + down_in[DOWN - 1, p].astype(F32)
-        )
-    finals = [
-        remote(
-            final_out.at[mate],
-            final_in.at[plane],
-            final_send.at[i],
-            final_recv.at[plane],
-            mate_ids[i],
-        )
-        for i, mate in enumerate(mates)
-    ]
-    for copy in finals:
-        copy.start()
-    final_in[plane] = final_out[plane]
+    gather(0)
+    serve(3)
+    serve(4)
+    serve_across(2)
+    send_round(0)
+    serve_across(3)
+    serve_across(4)
+    gather(1)
+    send_round(1)
+    gather(2)
+    send_round(2)
+    gather(3)
+    send_round(3)
+
+    values = plane_sum(0, 0)
+    for way in range(2):
+        values = arrived_sum(way, 0, values)
+    for b, value in enumerate(values):
+        final_out[b] = value
+    final = remote(
+        final_out.at[1 - core], final_in, final_send.at[0], final_recv.at[0], sibling
+    )
+    final.start()
 
     for peer in peers:
         remote(
@@ -365,16 +401,9 @@
         shrunk = shrunk + partial_sums[i]
     shrunk_ref[...] = shrunk.astype(BF16)
 
-    for step in range(STEPS):
-        first, count = slots_of_batch(step)
+    for batch in range(ROUNDS):
         for i, mate in enumerate(mates):
-            remote(
-                spread_out.at[i, pl.ds(first, count)],
-                spread_in.at[mate, pl.ds(first, count)],
-                spread_send.at[step, i],
-                spread_recv.at[step, mate],
-                mate_ids[i],
-            ).wait_recv()
+            spread(batch, i, mate, mate_ids[i]).wait_recv()
 
     get_inverse.wait()
 
@@ -401,30 +430,19 @@
         )
         bt_ref[:, pl.ds(pl.multiple_of(t * LANES, LANES), LANES)] = block.astype(BF16)
 
-    for i, mate in enumerate(mates):
-        remote(
-            final_out.at[mate],
-            final_in.at[mate],
-            final_send.at[i],
-            final_recv.at[mate],
-            mate_ids[i],
-        ).wait_recv()
-    for c in range(2):
-        for p in range(2):
-            total_ref[2 * c + p] = final_in[c, p] + final_in[2 + c, p]
-
-    for copy in core_copies + gups + gdowns + psums + spreads + finals:
+    total_ref[pl.ds(2 * core, 2)] = final_out[core]
+    final.wait_recv()
+    total_ref[pl.ds(2 * (1 - core), 2)] = final_in[...]
+
+    for copy in core_copies + y_copies + psums + spreads + [final]:
         copy.wait_send()
-    for way in hops:
-        for pair in way:
-            for copy in pair:
-                copy.wait_send()
+    for copy in list(hops.values()) + list(blocks.values()):
+        copy.wait_send()
 
 
 def exchange(adapters, table, counts, tokens, down, prior, grads):
-    smem = pl.BlockSpec(memory_space=pltpu.SMEM)
     vmem = pl.BlockSpec(memory_space=pltpu.VMEM)
-    hbm = pl.BlockSpec(memory_space=pl.ANY)
+    hbm = pl.BlockSpec(memory_space=pltpu.HBM)
     dma = pltpu.SemaphoreType.DMA
     chunk = (PLANE, PAD, LANES)
     return pl.pallas_call(
@@ -435,9 +453,13 @@
             jax.ShapeDtypeStruct((1, 128), jnp.int32),
             jax.ShapeDtypeStruct((4, PAD, LANES), F32),
         ),
-        in_specs=[smem, smem, smem, vmem, hbm, hbm, hbm, hbm],
+        in_specs=[hbm] * 7,
         out_specs=(vmem, vmem, vmem, vmem),
         scratch_shapes=[
+            pltpu.SMEM((64,), jnp.int32),
+            pltpu.SMEM((64,), jnp.int32),
+            pltpu.SMEM((64,), jnp.int32),
+            pltpu.VMEM((64,), jnp.int32),
             pltpu.VMEM((128, 1024), BF16),
             pltpu.VMEM((4, 64, 1024), BF16),
             pltpu.VMEM((240, 64), F32),
@@ -451,34 +473,30 @@
             pltpu.VMEM((Z * PLANE, 2, PAD, LANES), BF16),
             pltpu.VMEM((2 * STEPS, 2) + chunk, BF16),
             pltpu.VMEM((2 * STEPS, 2) + chunk, BF16),
-            pltpu.VMEM((2, 2) + chunk, F32),
-            pltpu.VMEM((UP, 2) + chunk, WIRE),
-            pltpu.VMEM((UP, 2) + chunk, WIRE),
-            pltpu.VMEM((DOWN, 2) + chunk, WIRE),
-            pltpu.VMEM((DOWN, 2) + chunk, WIRE),
-            pltpu.VMEM((DOWN, 4, PAD, LANES), BF16),
-            pltpu.VMEM((UP, 4, PAD, LANES), BF16),
+            pltpu.VMEM((Z, 2, 2, PAD, LANES), WIRE),
+            pltpu.VMEM((Z, 2, 2, PAD, LANES), WIRE),
+            pltpu.VMEM((2, DOWN, 2, 2, PAD, LANES), WIRE),
+            pltpu.VMEM((2, DOWN, 2, 2, PAD, LANES), WIRE),
+            pltpu.VMEM((2, DOWN, 4, PAD, LANES), BF16),
             pltpu.VMEM((PLANE - 1, Z, PAD, LANES), BF16),
             pltpu.VMEM((PLANE, Z, PAD, LANES), BF16),
-            pltpu.VMEM((PLANE, 2, PAD, LANES), F32),
-            pltpu.VMEM((PLANE, 2, PAD, LANES), F32),
+            pltpu.VMEM((2, 2, PAD, LANES), F32),
+            pltpu.VMEM((2, PAD, LANES), F32),
             pltpu.VMEM((TENSOR, 64, 128), F32),
             pltpu.VMEM((Z * PLANE, PAD, LANES), BF16),
-            dma((6,)),
+            dma((10,)),
             dma((2 * STEPS,)),
             dma((2 * STEPS,)),
-            dma((UP, 2)),
-            dma((UP, 2)),
-            dma((DOWN, 2)),
-            dma((DOWN, 2)),
-            dma((DOWN,)),
-            dma((DOWN,)),
-            dma((UP,)),
-            dma((UP,)),
-            dma((STEPS, PLANE - 1)),
-            dma((STEPS, PLANE)),
-            dma((PLANE - 1,)),
-            dma((PLANE,)),
+            dma((Z,)),
+            dma((Z,)),
+            dma((2, DOWN)),
+            dma((2, DOWN)),
+            dma((2, DOWN)),
+            dma((2, DOWN)),
+            dma((ROUNDS, PLANE - 1)),
+            dma((ROUNDS, PLANE)),
+            dma((1,)),
+            dma((1,)),
             dma((TENSOR - 1,)),
             dma((TENSOR,)),
         ],
@@ -491,7 +509,7 @@
             flops=2_000_000_000, bytes_accessed=8_000_000, transcendentals=0
         ),
         name="exchange",
-    )(adapters, table, counts, table.reshape(1, -1), tokens, down, prior, grads)
+    )(adapters, table, counts, tokens, down, prior, grads)
 
 
 def adam_kernel(total_ref, prior_ref, first_ref, second_ref, b_ref, m_ref, v_ref):

time: 56.2 us -> 49.9 us (0.89)
  Pallas kernels: 52.7 us -> 46.4 us
    pallas_call x1, Pallas kernels: 50.8 us -> 44.5 us  [exchange(): pl.pallas_call(exchange_kernel, out_shape=(jax.ShapeDtypeStruct((LANES, 1...]
where the time goes in v3:
time: 49.9 us; the launch traced here: 49.7 us
  Pallas kernels  46.4 us (93%)
  matrix products  1.49 us (3%)
  other arithmetic  1.1 us (2%)
  between operations  0.69 us (1%)
    pallas_call x1, Pallas kernels, exchange(): pl.pallas_call(exchange_kernel, out_shape=(jax.ShapeDtypeStruct((LANES, 1...  44.5 us
    pallas_call x1, Pallas kernels, adam(): pl.pallas_call(adam_kernel, out_shape=(jax.ShapeDtypeStruct((240, 64), F3...  1.9 us
    dot_general x1, matrix products, on_device(): jnp.einsum('rn,crg->ncg', shrunk, chosen.reshape(2, rank, width), preferr...  1.49 us
    convert_element_type x1, other arithmetic, on_device(): hidden = jnp.where((live[0] > 0)[:, None], gated, F32(0.0)).astype(BF16)  1.1 us

profile of v3, /device:TPU:1, one launch (start us, length us, event | category | flops | bytes accessed | tf_op | source)
XLA Modules:
  0.0 49.7 jit_solution(5256078103785936465)
XLA Ops:
  0.6 0.0 copy-start
  0.6 44.5 %exchange.1 = (bf16[128,1920]{1,0:T(8,128)(2,1)}, bf16[64,128]{1,0:T(8,128)(2,1)}, s32[1,128]{1,0:T(1,128)}, f32[4,32,128]{2,1,0:T(8,128)}) custom-call(s32[64]{0:T(128)} %bitcast.53, s32[64]{0:T(128)} %table_hbm.1, s32[64]{0:T(128)} %bitcast.54, bf16[128,1024]{1,0:T(8,128)(2,1)} %tokens_ref.1, bf16[4,64,1024]{2,1,0:T(8,128)(2,1)} %down_ref.1, ...), custom_call_target="tpu_custom_call" | custom-call | flops 2000000000 | bytes 8000000 | tf_op jit(solution)/shard_map/exchange/pallas_call | solution.py:448
  45.2 0.0 copy-start.1
  45.2 0.0 copy-done
  45.2 1.5 %fusion = f32[128,2,1920]{2,0,1:T(8,128)S(1)} fusion(bf16[2,64,1920]{2,1,0:T(8,128)(2,1)} %bitcast.44, bf16[128,2,1920]{2,1,0:T(2,128)(2,1)S(1)} %copy-done, bf16[64,128]{1,0:T(8,128)(2,1)} %get-tuple-element.16), kind=kOutput, calls=%fused_computation.1 | convolution fusion | flops 64389120 | bytes 3457024 | tf_op jit(solution)/shard_map/rn,crg->ncg/dot_general | solution.py:576
  46.7 0.0 copy-done.1
  46.7 1.1 %fusion.3 = bf16[128,1920]{1,0:T(8,128)(2,1)} fusion(f32[128,2,1920]{2,0,1:T(8,128)S(1)} %fusion, pred[128]{0:T(512)(128)(4,1)S(1)} %compare_bitcast_fusion), kind=kLoop, calls=%fused_computation.5 | loop fusion | flops 1720320 | bytes 2457728 | tf_op jit(solution)/shard_map/convert_element_type | solution.py:581
  47.8 1.9 %adam.1 = (f32[240,64]{1,0:T(8,128)}, f32[240,64]{1,0:T(8,128)}, f32[240,64]{1,0:T(8,128)}) custom-call(f32[4,32,128]{2,1,0:T(8,128)} %get-tuple-element.11.total_ref, f32[240,64]{1,0:T(8,128)} %bitcast.46, f32[240,64]{1,0:T(8,128)} %bitcast.47, f32[240,64]{1,0:T(8,128)} %bitcast.48), custom_call_target="tpu_custom_call" | custom-call | tf_op jit(solution)/shard_map/adam/pallas_call | solution.py:531
  (1 shorter events, 0.0 us)
Async XLA Ops:
  0.6 44.5 %copy-start = (bf16[128,2,1920]{2,1,0:T(2,128)(2,1)S(1)}, bf16[128,2,1920]{2,1,0:T(2,128)(2,1)}, u32[]{:S(2)}) copy-start(bf16[128,2,1920]{2,1,0:T(2,128)(2,1)} %param.11) | copy-start | bytes 2949124
  45.2 1.5 %copy-start.1 = (s32[1,128]{1,0:T(1,128)S(1)}, s32[1,128]{1,0:T(1,128)}, u32[]{:S(2)}) copy-start(s32[1,128]{1,0:T(1,128)} %get-tuple-element.15) | copy-start | bytes 1540

commit v4 on v3

--- a/solution.py
+++ b/solution.py
@@ -19,7 +19,7 @@
 MESH = pl.DeviceIdType.MESH
 Z = 16
 PLANE = 4
-TENSOR = 8
+WIDE = 4
 DOWN = Z // 2
 STEPS = Z // 2
 ROUNDS = Z // 4
@@ -67,6 +67,8 @@
     core_in,
     y_out,
     y_in,
+    early_out,
+    early_in,
     hop_out,
     hop_in,
     gathered,
@@ -75,12 +77,15 @@
     final_out,
     final_in,
     partial_sums,
+    pair_sums,
     natural,
     local_sem,
     core_send,
     core_recv,
     y_send,
     y_recv,
+    early_send,
+    early_recv,
     hop_send,
     hop_recv,
     gather_send,
@@ -89,6 +94,8 @@
     spread_recv,
     final_send,
     final_recv,
+    pair_send,
+    pair_recv,
     psum_send,
     psum_recv,
 ):
@@ -108,11 +115,13 @@
     across = (base + (1 - half) * 2 + core, tensor)
     mates = [lax.rem(plane + step, PLANE) for step in range(1, PLANE)]
     mate_ids = [(base + mate, tensor) for mate in mates]
-    peers = [lax.rem(tensor + step, TENSOR) for step in range(1, TENSOR)]
-    peer_ids = [(dp, peer) for peer in peers]
+    row, place_in_row = tensor // WIDE, tensor % WIDE
+    other_row = (dp, (1 - row) * WIDE + place_in_row)
+    peers = [lax.rem(place_in_row + step, WIDE) for step in range(1, WIDE)]
+    peer_ids = [(dp, row * WIDE + peer) for peer in peers]
 
     barrier = pltpu.get_barrier_semaphore()
-    everyone = [above, below, along(2), along(-2)] + mate_ids + peer_ids
+    everyone = [above, below, along(2), along(-2)] + mate_ids + peer_ids + [other_row]
     for device in everyone:
         pl.semaphore_signal(barrier, inc=1, device_id=device, device_id_type=MESH)
 
@@ -136,11 +145,12 @@
     wide[...] = jnp.zeros_like(wide)
     for copy in get_small:
         copy.wait()
-    row = lax.broadcasted_iota(jnp.int32, (64, 64), 0)
-    column = lax.broadcasted_iota(jnp.int32, (64, 64), 1)
+    owner_at = lax.broadcasted_iota(jnp.int32, (64, 64), 0)
+    block_at = lax.broadcasted_iota(jnp.int32, (64, 64), 1)
     table_rows = jnp.broadcast_to(table_row_ref[...].reshape(1, 64), (64, 64))
-    table_column = jnp.sum(jnp.where(row == column, table_rows, 0), axis=1, keepdims=True)
-    inverse_row[...] = jnp.sum(jnp.where(table_column == column, row, 0), axis=0, keepdims=True)
+    table_column = jnp.sum(jnp.where(owner_at == block_at, table_rows, 0), axis=1, keepdims=True)
+    found = jnp.where(table_column == block_at, owner_at, 0)
+    inverse_row[...] = jnp.sum(found, axis=0, keepdims=True)
     get_inverse = local(inverse_row, inverse, 5)
 
     get_prior.wait()
@@ -229,6 +239,7 @@
     y_copies = [
         remote(y_out.at[n], y_in.at[n], y_send.at[n], y_recv.at[n], across) for n in range(Z)
     ]
+    used_y = [y_copies[chunk_of(way, r)] for group in groups[1:] for way, r in group]
 
     def serve(group):
         for way, r in groups[group]:
@@ -244,11 +255,43 @@
             for b in range(2)
         ]
 
-    def serve_across(group):
-        for way, r in groups[group]:
+    early = {
+        (way, r): remote(
+            early_out.at[way, r - 7],
+            early_in.at[way, r - 7],
+            early_send.at[way, r - 7],
+            early_recv.at[way, r - 7],
+            along((1 if way == 0 else -1) * (r - 6)),
+        )
+        for way, r in groups[0]
+    }
+
+    def send_early():
+        for way, r in groups[0]:
+            core_copies[chunk_of(way, r)].wait_recv()
+            for side in range(2):
+                for b, value in enumerate(chip_sum(way, r, side)):
+                    early_out[way, r - 7, :, 2 * side + b] = value.astype(WIRE)
+            early[way, r].start()
+
+    def line_sum(way, r, side):
+        values = chip_sum(way, r, side)
+        for child in (7, 8) if r == 6 else ():
+            if (way, child) in early:
+                values = [
+                    value + early_in[way, child - 7, :, 2 * side + b].astype(F32)
+                    for b, value in enumerate(values)
+                ]
+        return values
+
+    def serve_across(r):
+        for way in range(2 if r else 1):
             n = chunk_of(way, r)
             core_copies[n].wait_recv()
-            for b, value in enumerate(chip_sum(way, r, 1 - half)):
+            for child in (7, 8) if r == 6 else ():
+                if (way, child) in early:
+                    early[way, child].wait_recv()
+            for b, value in enumerate(line_sum(way, r, 1 - half)):
                 y_out[n, :, b] = value.astype(WIRE)
             y_copies[n].start()
 
@@ -257,30 +300,50 @@
 
     get_own.wait()
     turn(own_half, own_terms)
-    serve_across(0)
+    send_early()
     serve(2)
-    serve_across(1)
+    serve_across(5)
+    serve_across(4)
+    serve(3)
+    serve(4)
+    serve_across(3)
 
     get_down.wait()
     get_tokens.wait()
-    partial_sums[tensor] = lax.dot_general(
+    partial_sums[row] = lax.dot_general(
         down_in_all[adapters_ref[dp]],
         tokens_in[...],
         (((1,), (1,)), ((), ())),
         preferred_element_type=F32,
     )
-    psums = [
+    pair = remote(
+        partial_sums.at[row], partial_sums.at[row], pair_send.at[0], pair_recv.at[row], other_row
+    )
+    pair.start()
+
+    def psum(i, source):
+        return remote(
+            pair_sums.at[source],
+            pair_sums.at[source],
+            psum_send.at[i],
+            psum_recv.at[source],
+            peer_ids[i],
+        )
+
+    psums = [psum(i, place_in_row) for i in range(WIDE - 1)]
+
+    def sum_rows():
         remote(
-            partial_sums.at[tensor],
-            partial_sums.at[tensor],
-            psum_send.at[i],
-            psum_recv.at[tensor],
-            device,
-        )
-        for i, device in enumerate(peer_ids)
-    ]
-    for copy in psums:
-        copy.start()
+            partial_sums.at[1 - row],
+            partial_sums.at[1 - row],
+            pair_send.at[0],
+            pair_recv.at[1 - row],
+            other_row,
+        ).wait_recv()
+        pair_sums[place_in_row] = partial_sums[0] + partial_sums[1]
+        for copy in psums:
+            copy.start()
+
     plane_adapters = [adapters_ref[base + lax.rem(plane + step, PLANE)] for step in range(PLANE)]
     live_ref[...] = (
         lax.broadcasted_iota(jnp.int32, (1, 128), 1) < counts_ref[dp]
@@ -294,14 +357,14 @@
             hop_recv.at[way, r - 1],
             along((1 if way == 0 else -1) * (1 if r % 2 else 2)),
         )
-        for group in groups[:-1]
+        for group in groups[1:-1]
         for way, r in group
     }
 
     def plane_sum(way, r):
         n = chunk_of(way, r)
         y_copies[n].wait_recv()
-        return [value + y_in[n, :, b].astype(F32) for b, value in enumerate(chip_sum(way, r, half))]
+        return [value + y_in[n, :, b].astype(F32) for b, value in enumerate(line_sum(way, r, half))]
 
     def arrived_sum(way, r, values):
         for child in (r + 1, r + 2):
@@ -345,12 +408,14 @@
         for i in range(PLANE - 1):
             spread_out[i, slot] = choose(block, plane_adapters[i + 1])
 
-    def gather(batch):
+    def gather_pass(batch):
         for way in range(2):
             if (way, 2 * batch + 2) in blocks:
                 blocks[way, 2 * batch + 2].wait_recv()
         if batch + 1 < ROUNDS:
             pass_round(batch + 1)
+
+    def gather_spread(batch):
         if batch == 0:
             place(mine[...], 0)
         for r in (2 * batch + 1, 2 * batch + 2):
@@ -364,18 +429,21 @@
             copy.start()
             spreads.append(copy)
 
-    gather(0)
-    serve(3)
-    serve(4)
+    gather_pass(0)
+    serve_across(6)
     serve_across(2)
-    send_round(0)
-    serve_across(3)
-    serve_across(4)
-    gather(1)
+    serve_across(1)
+    serve_across(0)
+    gather_pass(1)
     send_round(1)
-    gather(2)
+    gather_spread(0)
+    gather_pass(2)
+    gather_spread(1)
+    sum_rows()
     send_round(2)
-    gather(3)
+    gather_pass(3)
+    gather_spread(2)
+    gather_spread(3)
     send_round(3)
 
     values = plane_sum(0, 0)
@@ -388,17 +456,11 @@
     )
     final.start()
 
-    for peer in peers:
-        remote(
-            partial_sums.at[peer],
-            partial_sums.at[peer],
-            psum_send.at[0],
-            psum_recv.at[peer],
-            peer_ids[0],
-        ).wait_recv()
-    shrunk = partial_sums[0]
-    for i in range(1, TENSOR):
-        shrunk = shrunk + partial_sums[i]
+    for i, peer in enumerate(peers):
+        psum(i, peer).wait_recv()
+    shrunk = pair_sums[0]
+    for i in range(1, WIDE):
+        shrunk = shrunk + pair_sums[i]
     shrunk_ref[...] = shrunk.astype(BF16)
 
     for batch in range(ROUNDS):
@@ -434,9 +496,9 @@
     final.wait_recv()
     total_ref[pl.ds(2 * (1 - core), 2)] = final_in[...]
 
-    for copy in core_copies + y_copies + psums + spreads + [final]:
+    for copy in core_copies + used_y + psums + spreads + [pair, final]:
         copy.wait_send()
-    for copy in list(hops.values()) + list(blocks.values()):
+    for copy in list(early.values()) + list(hops.values()) + list(blocks.values()):
         copy.wait_send()
 
 
@@ -475,6 +537,8 @@
             pltpu.VMEM((2 * STEPS, 2) + chunk, BF16),
             pltpu.VMEM((Z, 2, 2, PAD, LANES), WIRE),
             pltpu.VMEM((Z, 2, 2, PAD, LANES), WIRE),
+            pltpu.VMEM((2, 2) + (2,) + chunk, WIRE),
+            pltpu.VMEM((2, 2) + (2,) + chunk, WIRE),
             pltpu.VMEM((2, DOWN, 2, 2, PAD, LANES), WIRE),
             pltpu.VMEM((2, DOWN, 2, 2, PAD, LANES), WIRE),
             pltpu.VMEM((2, DOWN, 4, PAD, LANES), BF16),
@@ -482,13 +546,16 @@
             pltpu.VMEM((PLANE, Z, PAD, LANES), BF16),
             pltpu.VMEM((2, 2, PAD, LANES), F32),
             pltpu.VMEM((2, PAD, LANES), F32),
-            pltpu.VMEM((TENSOR, 64, 128), F32),
+            pltpu.VMEM((2, 64, 128), F32),
+            pltpu.VMEM((WIDE, 64, 128), F32),
             pltpu.VMEM((Z * PLANE, PAD, LANES), BF16),
             dma((10,)),
             dma((2 * STEPS,)),
             dma((2 * STEPS,)),
             dma((Z,)),
             dma((Z,)),
+            dma((2, 2)),
+            dma((2, 2)),
             dma((2, DOWN)),
             dma((2, DOWN)),
             dma((2, DOWN)),
@@ -497,8 +564,10 @@
             dma((ROUNDS, PLANE)),
             dma((1,)),
             dma((1,)),
-            dma((TENSOR - 1,)),
-            dma((TENSOR,)),
+            dma((1,)),
+            dma((2,)),
+            dma((WIDE - 1,)),
+            dma((WIDE,)),
         ],
         compiler_params=pltpu.CompilerParams(
             collective_id=0,

time: 49.9 us -> 48.4 us (0.970)
  Pallas kernels: 46.4 us -> 45 us
    pallas_call x1, Pallas kernels: 44.5 us -> 43.1 us  [exchange(): pl.pallas_call(exchange_kernel, out_shape=(jax.ShapeDtypeStruct((LANES, 1...]
where the time goes in v4:
time: 48.4 us; the launch traced here: 48.3 us
  Pallas kernels  45 us (93%)
  matrix products  1.49 us (3%)
  other arithmetic  1.1 us (2%)
  between operations  0.69 us (1%)
    pallas_call x1, Pallas kernels, exchange(): pl.pallas_call(exchange_kernel, out_shape=(jax.ShapeDtypeStruct((LANES, 1...  43.1 us
    pallas_call x1, Pallas kernels, adam(): pl.pallas_call(adam_kernel, out_shape=(jax.ShapeDtypeStruct((240, 64), F3...  1.9 us
    dot_general x1, matrix products, on_device(): jnp.einsum('rn,crg->ncg', shrunk, chosen.reshape(2, rank, width), preferr...  1.49 us
    convert_element_type x1, other arithmetic, on_device(): hidden = jnp.where((live[0] > 0)[:, None], gated, F32(0.0)).astype(BF16)  1.1 us

profile of v4, /device:TPU:1, one launch (start us, length us, event | category | flops | bytes accessed | tf_op | source)
XLA Modules:
  0.0 48.3 jit_solution(8338390250384297239)
XLA Ops:
  0.6 0.0 copy-start
  0.6 43.1 %exchange.1 = (bf16[128,1920]{1,0:T(8,128)(2,1)}, bf16[64,128]{1,0:T(8,128)(2,1)}, s32[1,128]{1,0:T(1,128)}, f32[4,32,128]{2,1,0:T(8,128)}) custom-call(s32[64]{0:T(128)} %bitcast.53, s32[64]{0:T(128)} %table_hbm.1, s32[64]{0:T(128)} %bitcast.54, bf16[128,1024]{1,0:T(8,128)(2,1)} %tokens_ref.1, bf16[4,64,1024]{2,1,0:T(8,128)(2,1)} %down_ref.1, ...), custom_call_target="tpu_custom_call" | custom-call | flops 2000000000 | bytes 8000000 | tf_op jit(solution)/shard_map/exchange/pallas_call | solution.py:510
  43.7 0.0 copy-start.1
  43.7 0.0 copy-done
  43.7 1.5 %fusion = f32[128,2,1920]{2,0,1:T(8,128)S(1)} fusion(bf16[2,64,1920]{2,1,0:T(8,128)(2,1)} %bitcast.44, bf16[128,2,1920]{2,1,0:T(2,128)(2,1)S(1)} %copy-done, bf16[64,128]{1,0:T(8,128)(2,1)} %get-tuple-element.16), kind=kOutput, calls=%fused_computation.1 | convolution fusion | flops 64389120 | bytes 3457024 | tf_op jit(solution)/shard_map/rn,crg->ncg/dot_general | solution.py:645
  45.2 0.0 copy-done.1
  45.2 1.1 %fusion.3 = bf16[128,1920]{1,0:T(8,128)(2,1)} fusion(f32[128,2,1920]{2,0,1:T(8,128)S(1)} %fusion, pred[128]{0:T(512)(128)(4,1)S(1)} %compare_bitcast_fusion), kind=kLoop, calls=%fused_computation.5 | loop fusion | flops 1720320 | bytes 2457728 | tf_op jit(solution)/shard_map/convert_element_type | solution.py:650
  46.3 1.9 %adam.1 = (f32[240,64]{1,0:T(8,128)}, f32[240,64]{1,0:T(8,128)}, f32[240,64]{1,0:T(8,128)}) custom-call(f32[4,32,128]{2,1,0:T(8,128)} %get-tuple-element.11.total_ref, f32[240,64]{1,0:T(8,128)} %bitcast.46, f32[240,64]{1,0:T(8,128)} %bitcast.47, f32[240,64]{1,0:T(8,128)} %bitcast.48), custom_call_target="tpu_custom_call" | custom-call | tf_op jit(solution)/shard_map/adam/pallas_call | solution.py:600
  (1 shorter events, 0.0 us)
Async XLA Ops:
  0.6 43.1 %copy-start = (bf16[128,2,1920]{2,1,0:T(2,128)(2,1)S(1)}, bf16[128,2,1920]{2,1,0:T(2,128)(2,1)}, u32[]{:S(2)}) copy-start(bf16[128,2,1920]{2,1,0:T(2,128)(2,1)} %param.11) | copy-start | bytes 2949124
  43.7 1.5 %copy-start.1 = (s32[1,128]{1,0:T(1,128)S(1)}, s32[1,128]{1,0:T(1,128)}, u32[]{:S(2)}) copy-start(s32[1,128]{1,0:T(1,128)} %get-tuple-element.15) | copy-start | bytes 1540

commit v5 on v4

--- a/solution.py
+++ b/solution.py
@@ -57,6 +57,7 @@
     prior_in,
     wide,
     mine,
+    lag,
     inverse_row,
     inverse,
     own_half,
@@ -79,6 +80,7 @@
     partial_sums,
     pair_sums,
     natural,
+    factor,
     local_sem,
     core_send,
     core_recv,
@@ -161,26 +163,28 @@
             ]
     mine[...] = wide[...].astype(BF16)
 
-    def picker(q):
-        window = jnp.minimum((120 * q) // LANES * LANES, 1920 - 2 * LANES)
-        offset = 120 * q - window
-        row = lax.broadcasted_iota(jnp.int32, (PLANE * PAD, 2 * LANES), 0)
-        column = lax.broadcasted_iota(jnp.int32, (PLANE * PAD, 2 * LANES), 1)
-        hit = (column == offset + row - 2 * (row // PAD)) & (row % PAD < FB)
-        return pl.multiple_of(window, LANES), jnp.where(hit, F32(1.0), F32(0.0)).astype(BF16)
+    turn_row = lax.broadcasted_iota(jnp.int32, (PLANE * PAD, 2 * LANES), 0)
+    turn_column = lax.broadcasted_iota(jnp.int32, (PLANE * PAD, 2 * LANES), 1)
+    lag[...] = jnp.where(turn_row % PAD < FB, turn_column - turn_row + 2 * (turn_row // PAD), -1)
 
     def turn(half, terms):
-        @pl.loop(0, Z, unroll=2)
+        @pl.loop(0, Z, unroll=4)
         def _(q):
-            window, pick = picker(q)
+            window = pl.multiple_of(
+                jnp.minimum((120 * q) // LANES * LANES, 1920 - 2 * LANES), LANES
+            )
+            offset = 120 * q - window
+            pick = jnp.where(lag[...] == offset, F32(1.0), F32(0.0)).astype(BF16)
+            block = lax.dot_general(
+                pick,
+                half[:, :, pl.ds(window, 2 * LANES)].reshape(2 * LANES, 2 * LANES),
+                (((1,), (1,)), ((), ())),
+                preferred_element_type=F32,
+            ).astype(BF16)
             for p in range(2):
-                block = lax.dot_general(
-                    pick,
-                    half[p, :, pl.ds(window, 2 * LANES)],
-                    (((1,), (1,)), ((), ())),
-                    preferred_element_type=F32,
+                terms[pl.ds(PLANE * q, PLANE), p] = block[:, p * LANES : (p + 1) * LANES].reshape(
+                    PLANE, PAD, LANES
                 )
-                terms[pl.ds(PLANE * q, PLANE), p] = block.reshape(PLANE, PAD, LANES).astype(BF16)
 
     get_other.wait()
     turn(other_half, other_terms)
@@ -306,7 +310,6 @@
     serve_across(4)
     serve(3)
     serve(4)
-    serve_across(3)
 
     get_down.wait()
     get_tokens.wait()
@@ -431,6 +434,7 @@
 
     gather_pass(0)
     serve_across(6)
+    serve_across(3)
     serve_across(2)
     serve_across(1)
     serve_across(0)
@@ -446,16 +450,6 @@
     gather_spread(3)
     send_round(3)
 
-    values = plane_sum(0, 0)
-    for way in range(2):
-        values = arrived_sum(way, 0, values)
-    for b, value in enumerate(values):
-        final_out[b] = value
-    final = remote(
-        final_out.at[1 - core], final_in, final_send.at[0], final_recv.at[0], sibling
-    )
-    final.start()
-
     for i, peer in enumerate(peers):
         psum(i, peer).wait_recv()
     shrunk = pair_sums[0]
@@ -490,12 +484,24 @@
             (((0,), (0,)), ((), ())),
             preferred_element_type=F32,
         )
-        bt_ref[:, pl.ds(pl.multiple_of(t * LANES, LANES), LANES)] = block.astype(BF16)
+        factor[:, pl.ds(pl.multiple_of(t * LANES, LANES), LANES)] = block.astype(BF16)
+    put_factor = local(factor, bt_ref, 10)
+
+    values = plane_sum(0, 0)
+    for way in range(2):
+        values = arrived_sum(way, 0, values)
+    for b, value in enumerate(values):
+        final_out[b] = value
+    final = remote(
+        final_out.at[1 - core], final_in, final_send.at[0], final_recv.at[0], sibling
+    )
+    final.start()
 
     total_ref[pl.ds(2 * core, 2)] = final_out[core]
     final.wait_recv()
     total_ref[pl.ds(2 * (1 - core), 2)] = final_in[...]
 
+    put_factor.wait()
     for copy in core_copies + used_y + psums + spreads + [pair, final]:
         copy.wait_send()
     for copy in list(early.values()) + list(hops.values()) + list(blocks.values()):
@@ -516,7 +522,7 @@
             jax.ShapeDtypeStruct((4, PAD, LANES), F32),
         ),
         in_specs=[hbm] * 7,
-        out_specs=(vmem, vmem, vmem, vmem),
+        out_specs=(hbm, vmem, vmem, vmem),
         scratch_shapes=[
             pltpu.SMEM((64,), jnp.int32),
             pltpu.SMEM((64,), jnp.int32),
@@ -527,6 +533,7 @@
             pltpu.VMEM((240, 64), F32),
             pltpu.VMEM((4, PAD, LANES), F32),
             pltpu.VMEM((4, PAD, LANES), BF16),
+            pltpu.VMEM((PLANE * PAD, 2 * LANES), jnp.int32),
             pltpu.VMEM((1, 64), jnp.int32),
             pltpu.SMEM((1, 64), jnp.int32),
             pltpu.VMEM((2, LANES, 1920), BF16),
@@ -549,7 +556,8 @@
             pltpu.VMEM((2, 64, 128), F32),
             pltpu.VMEM((WIDE, 64, 128), F32),
             pltpu.VMEM((Z * PLANE, PAD, LANES), BF16),
-            dma((10,)),
+            pltpu.VMEM((LANES, 1920), BF16),
+            dma((11,)),
             dma((2 * STEPS,)),
             dma((2 * STEPS,)),
             dma((Z,)),

time: 48.4 us -> 47.8 us (0.988)
  Pallas kernels: 45 us -> 44.4 us
    pallas_call x1, Pallas kernels: 43.1 us -> 42.5 us  [exchange(): pl.pallas_call(exchange_kernel, out_shape=(jax.ShapeDtypeStruct((LANES, 1...]
where the time goes in v5:
time: 47.8 us; the launch traced here: 47.7 us
  Pallas kernels  44.4 us (93%)
  matrix products  1.49 us (3%)
  other arithmetic  1.1 us (2%)
  between operations  0.69 us (1%)
    pallas_call x1, Pallas kernels, exchange(): pl.pallas_call(exchange_kernel, out_shape=(jax.ShapeDtypeStruct((LANES, 1...  42.5 us
    pallas_call x1, Pallas kernels, adam(): pl.pallas_call(adam_kernel, out_shape=(jax.ShapeDtypeStruct((240, 64), F3...  1.9 us
    dot_general x1, matrix products, on_device(): jnp.einsum('rn,crg->ncg', shrunk, chosen.reshape(2, rank, width), preferr...  1.49 us
    convert_element_type x1, other arithmetic, on_device(): hidden = jnp.where((live[0] > 0)[:, None], gated, F32(0.0)).astype(BF16)  1.1 us

profile of v5, /device:TPU:1, one launch (start us, length us, event | category | flops | bytes accessed | tf_op | source)
XLA Modules:
  0.0 47.7 jit_solution(8175053320981004074)
XLA Ops:
  0.6 0.0 copy-start
  0.6 42.5 %exchange.1 = (bf16[128,1920]{1,0:T(8,128)(2,1)}, bf16[64,128]{1,0:T(8,128)(2,1)}, s32[1,128]{1,0:T(1,128)}, f32[4,32,128]{2,1,0:T(8,128)}) custom-call(s32[64]{0:T(128)} %bitcast.53, s32[64]{0:T(128)} %table_hbm.1, s32[64]{0:T(128)} %bitcast.54, bf16[128,1024]{1,0:T(8,128)(2,1)} %tokens_ref.1, bf16[4,64,1024]{2,1,0:T(8,128)(2,1)} %down_ref.1, ...), custom_call_target="tpu_custom_call" | custom-call | flops 2000000000 | bytes 8000000 | tf_op jit(solution)/shard_map/exchange/pallas_call | solution.py:516
  43.1 0.0 copy-start.1
  43.1 0.0 copy-done
  43.1 1.5 %fusion = f32[128,2,1920]{2,0,1:T(8,128)S(1)} fusion(bf16[2,64,1920]{2,1,0:T(8,128)(2,1)} %bitcast.44, bf16[128,2,1920]{2,1,0:T(2,128)(2,1)S(1)} %copy-done, bf16[64,128]{1,0:T(8,128)(2,1)} %get-tuple-element.16), kind=kOutput, calls=%fused_computation.1 | convolution fusion | flops 64389120 | bytes 3457024 | tf_op jit(solution)/shard_map/rn,crg->ncg/dot_general | solution.py:653
  44.6 0.0 copy-done.1
  44.7 1.1 %fusion.3 = bf16[128,1920]{1,0:T(8,128)(2,1)} fusion(f32[128,2,1920]{2,0,1:T(8,128)S(1)} %fusion, pred[128]{0:T(512)(128)(4,1)S(1)} %compare_bitcast_fusion), kind=kLoop, calls=%fused_computation.5 | loop fusion | flops 1720320 | bytes 2457728 | tf_op jit(solution)/shard_map/convert_element_type | solution.py:658
  45.8 1.9 %adam.1 = (f32[240,64]{1,0:T(8,128)}, f32[240,64]{1,0:T(8,128)}, f32[240,64]{1,0:T(8,128)}) custom-call(f32[4,32,128]{2,1,0:T(8,128)} %get-tuple-element.11.total_ref, f32[240,64]{1,0:T(8,128)} %bitcast.46, f32[240,64]{1,0:T(8,128)} %bitcast.47, f32[240,64]{1,0:T(8,128)} %bitcast.48), custom_call_target="tpu_custom_call" | custom-call | tf_op jit(solution)/shard_map/adam/pallas_call | solution.py:608
  (1 shorter events, 0.0 us)
Async XLA Ops:
  0.6 42.5 %copy-start = (bf16[128,2,1920]{2,1,0:T(2,128)(2,1)S(1)}, bf16[128,2,1920]{2,1,0:T(2,128)(2,1)}, u32[]{:S(2)}) copy-start(bf16[128,2,1920]{2,1,0:T(2,128)(2,1)} %param.11) | copy-start | bytes 2949124
  43.1 1.5 %copy-start.1 = (s32[1,128]{1,0:T(1,128)S(1)}, s32[1,128]{1,0:T(1,128)}, u32[]{:S(2)}) copy-start(s32[1,128]{1,0:T(1,128)} %get-tuple-element.15) | copy-start | bytes 1540

commit v6 on v5

--- a/solution.py
+++ b/solution.py
@@ -144,25 +144,6 @@
     get_down = local(down_ref, down_in_all, 3)
     get_tokens = local(tokens_ref, tokens_in, 4)
 
-    wide[...] = jnp.zeros_like(wide)
-    for copy in get_small:
-        copy.wait()
-    owner_at = lax.broadcasted_iota(jnp.int32, (64, 64), 0)
-    block_at = lax.broadcasted_iota(jnp.int32, (64, 64), 1)
-    table_rows = jnp.broadcast_to(table_row_ref[...].reshape(1, 64), (64, 64))
-    table_column = jnp.sum(jnp.where(owner_at == block_at, table_rows, 0), axis=1, keepdims=True)
-    found = jnp.where(table_column == block_at, owner_at, 0)
-    inverse_row[...] = jnp.sum(found, axis=0, keepdims=True)
-    get_inverse = local(inverse_row, inverse, 5)
-
-    get_prior.wait()
-    for a in range(4):
-        for c in range(2):
-            wide[a, pl.ds(0, FB), pl.ds(64 * c, 64)] = prior_in[
-                pl.ds(2 * FB * a + c, FB, stride=2), :
-            ]
-    mine[...] = wide[...].astype(BF16)
-
     turn_row = lax.broadcasted_iota(jnp.int32, (PLANE * PAD, 2 * LANES), 0)
     turn_column = lax.broadcasted_iota(jnp.int32, (PLANE * PAD, 2 * LANES), 1)
     lag[...] = jnp.where(turn_row % PAD < FB, turn_column - turn_row + 2 * (turn_row // PAD), -1)
@@ -189,6 +170,18 @@
     get_other.wait()
     turn(other_half, other_terms)
 
+    wide[...] = jnp.zeros_like(wide)
+    get_prior.wait()
+    for a in range(4):
+        for c in range(2):
+            wide[a, pl.ds(0, FB), pl.ds(64 * c, 64)] = prior_in[
+                pl.ds(2 * FB * a + c, FB, stride=2), :
+            ]
+    mine[...] = wide[...].astype(BF16)
+
+    for copy in get_small:
+        copy.wait()
+
     pl.semaphore_wait(barrier, len(everyone))
 
     def remote(src, dst, send, recv, device):
@@ -310,6 +303,14 @@
     serve_across(4)
     serve(3)
     serve(4)
+
+    owner_at = lax.broadcasted_iota(jnp.int32, (64, 64), 0)
+    block_at = lax.broadcasted_iota(jnp.int32, (64, 64), 1)
+    table_rows = jnp.broadcast_to(table_row_ref[...].reshape(1, 64), (64, 64))
+    table_column = jnp.sum(jnp.where(owner_at == block_at, table_rows, 0), axis=1, keepdims=True)
+    found = jnp.where(table_column == block_at, owner_at, 0)
+    inverse_row[...] = jnp.sum(found, axis=0, keepdims=True)
+    get_inverse = local(inverse_row, inverse, 5)
 
     get_down.wait()
     get_tokens.wait()

time: 47.8 us -> 47.8 us (level)
  no operation moved by 1% of the time
where the time goes in v6:
time: 47.8 us; the launch traced here: 47.6 us
  Pallas kernels  44.3 us (93%)
  matrix products  1.49 us (3%)
  other arithmetic  1.1 us (2%)
  between operations  0.69 us (1%)
    pallas_call x1, Pallas kernels, exchange(): pl.pallas_call(exchange_kernel, out_shape=(jax.ShapeDtypeStruct((LANES, 1...  42.4 us
    pallas_call x1, Pallas kernels, adam(): pl.pallas_call(adam_kernel, out_shape=(jax.ShapeDtypeStruct((240, 64), F3...  1.9 us
    dot_general x1, matrix products, on_device(): jnp.einsum('rn,crg->ncg', shrunk, chosen.reshape(2, rank, width), preferr...  1.49 us
    convert_element_type x1, other arithmetic, on_device(): hidden = jnp.where((live[0] > 0)[:, None], gated, F32(0.0)).astype(BF16)  1.1 us

profile of v6, /device:TPU:1, one launch (start us, length us, event | category | flops | bytes accessed | tf_op | source)
XLA Modules:
  0.0 47.6 jit_solution(11038284105368901737)
XLA Ops:
  0.6 0.0 copy-start
  0.6 42.4 %exchange.1 = (bf16[128,1920]{1,0:T(8,128)(2,1)}, bf16[64,128]{1,0:T(8,128)(2,1)}, s32[1,128]{1,0:T(1,128)}, f32[4,32,128]{2,1,0:T(8,128)}) custom-call(s32[64]{0:T(128)} %bitcast.53, s32[64]{0:T(128)} %table_hbm.1, s32[64]{0:T(128)} %bitcast.54, bf16[128,1024]{1,0:T(8,128)(2,1)} %tokens_ref.1, bf16[4,64,1024]{2,1,0:T(8,128)(2,1)} %down_ref.1, ...), custom_call_target="tpu_custom_call" | custom-call | flops 2000000000 | bytes 8000000 | tf_op jit(solution)/shard_map/exchange/pallas_call | solution.py:517
  43.1 0.0 copy-start.1
  43.1 0.0 copy-done
  43.1 1.5 %fusion = f32[128,2,1920]{2,0,1:T(8,128)S(1)} fusion(bf16[2,64,1920]{2,1,0:T(8,128)(2,1)} %bitcast.44, bf16[128,2,1920]{2,1,0:T(2,128)(2,1)S(1)} %copy-done, bf16[64,128]{1,0:T(8,128)(2,1)} %get-tuple-element.16), kind=kOutput, calls=%fused_computation.1 | convolution fusion | flops 64389120 | bytes 3457024 | tf_op jit(solution)/shard_map/rn,crg->ncg/dot_general | solution.py:654
  44.6 0.0 copy-done.1
  44.6 1.1 %fusion.3 = bf16[128,1920]{1,0:T(8,128)(2,1)} fusion(f32[128,2,1920]{2,0,1:T(8,128)S(1)} %fusion, pred[128]{0:T(512)(128)(4,1)S(1)} %compare_bitcast_fusion), kind=kLoop, calls=%fused_computation.5 | loop fusion | flops 1720320 | bytes 2457728 | tf_op jit(solution)/shard_map/convert_element_type | solution.py:659
  45.7 1.9 %adam.1 = (f32[240,64]{1,0:T(8,128)}, f32[240,64]{1,0:T(8,128)}, f32[240,64]{1,0:T(8,128)}) custom-call(f32[4,32,128]{2,1,0:T(8,128)} %get-tuple-element.11.total_ref, f32[240,64]{1,0:T(8,128)} %bitcast.46, f32[240,64]{1,0:T(8,128)} %bitcast.47, f32[240,64]{1,0:T(8,128)} %bitcast.48), custom_call_target="tpu_custom_call" | custom-call | tf_op jit(solution)/shard_map/adam/pallas_call | solution.py:609
  (1 shorter events, 0.0 us)
Async XLA Ops:
  0.6 42.4 %copy-start = (bf16[128,2,1920]{2,1,0:T(2,128)(2,1)S(1)}, bf16[128,2,1920]{2,1,0:T(2,128)(2,1)}, u32[]{:S(2)}) copy-start(bf16[128,2,1920]{2,1,0:T(2,128)(2,1)} %param.11) | copy-start | bytes 2949124
  43.1 1.5 %copy-start.1 = (s32[1,128]{1,0:T(1,128)S(1)}, s32[1,128]{1,0:T(1,128)}, u32[]{:S(2)}) copy-start(s32[1,128]{1,0:T(1,128)} %get-tuple-element.15) | copy-start | bytes 1540
